TPU v7x, 128 devices: a whole 4x4x4 slice. The times are simulated.
128 devices in a mesh: growth: 4 (over x), lateral: 32 (over z, y, core).
Axes of the slice: x: 4, y: 4, z: 4, core: 2. Of those that a mesh axis runs over, the one named last changes fastest.
Arguments:
- phase_now: float32 [128, 1024, 128], P('growth', 'lateral'), may hold values from -1 to 1
- phase_old: float32 [128, 1024, 128], P('growth', 'lateral'), may hold values from -1 to 1
- solute: float32 [128, 1024, 128], P('growth', 'lateral'), may hold values from 0.5 to 1.5
- iface_blocks: int32 [4, 32, 6], P('growth', 'lateral'), may hold values from 0 to 7, as said below
- iface_count: int32 [4, 32], P('growth', 'lateral'), may hold values from 1 to 6, as said below
Outputs:
- solute_next: float32 [128, 1024, 128], P('growth', 'lateral')
Inputs may be any that keep to these rules, and one draw needn't show every extreme that they name: `iface_blocks`: in each row of a device's list all 6 ids differ; the first iface_count of them name its interface blocks. `iface_count`: the devices at lateral indices 2j and 2j+1 with the same growth index hold at most 8 interface blocks together; in every growth row one such pair holds exactly 8, one device of it 6.
All inputs are finite; a program needn't handle non-finite values.
Results may differ from a plain program's by a relative error of at most 0.00013.
Values sent between devices are 32-bit elements; how exact they have to be, the bound alone decides.
A program may use at most 64 MiB of HBM per device.

v0:
```python
import jax
import jax.numpy as jnp
from jax import lax
from jax.sharding import PartitionSpec as P

BZ = 4


DIFF_LIQ = 1.0
DIFF_SOL = 0.1
LATERAL_RATE = 0.1
VERTICAL_RATE = 400.0
TRAPPING = 0.5
PARTITION = 0.3
ANISOTROPY = 0.3
REGULAR = 0.25


def with_halo(cells, sides, width):
    for axis, dim in sides:
        count = lax.axis_size(axis)
        ends = count - 1
        head = lax.slice_in_dim(cells, 0, width, axis=dim)
        tail = lax.slice_in_dim(cells, cells.shape[dim] - width, cells.shape[dim], axis=dim)
        cells = jnp.concatenate(
            [
                lax.ppermute(tail, axis, [(i, (i + 1) % count) for i in range(ends)]),
                cells,
                lax.ppermute(head, axis, [((i + 1) % count, i) for i in range(ends)]),
            ],
            axis=dim,
        )
    return cells


def diffusivity(phase_values):
    return DIFF_LIQ * (1.0 - phase_values) * 0.5 + DIFF_SOL * (1.0 + phase_values) * 0.5


def interface_flux(features):
    grad_x = features[0]
    grad_y = features[1]
    grad_z = features[2]
    norm_sq = grad_x * grad_x + grad_y * grad_y + grad_z * grad_z + REGULAR
    quartic = (
        grad_x * grad_x * grad_x * grad_x
        + grad_y * grad_y * grad_y * grad_y
        + grad_z * grad_z * grad_z * grad_z
    )
    anisotropic = 1.0 + ANISOTROPY * (4.0 * quartic / (norm_sq * norm_sq) - 3.0)
    strength = (
        TRAPPING
        * (1.0 + (1.0 - PARTITION) * features[4])
        * features[3]
        * anisotropic
        / jnp.sqrt(norm_sq)
    )
    return jnp.stack([strength * grad_x, strength * grad_y, strength * grad_z])


def lower_rows(values, stride, fill_value):
    head_block = jnp.full(
        values.shape[:-3] + (stride,) + values.shape[-2:], fill_value, values.dtype
    )
    return jnp.concatenate([head_block, values[..., :-stride, :, :]], axis=-3)


def upper_rows(values, stride, fill_value):
    tail_block = jnp.full(
        values.shape[:-3] + (stride,) + values.shape[-2:], fill_value, values.dtype
    )
    return jnp.concatenate([values[..., stride:, :, :], tail_block], axis=-3)


def local_solve(below_coef, diagonal, above_coef, right_sides):
    slab_depth = diagonal.shape[0]
    stride = 1
    while stride < slab_depth:
        left_ratio = below_coef / lower_rows(diagonal, stride, 1.0)
        right_ratio = above_coef / upper_rows(diagonal, stride, 1.0)
        diagonal = (
            diagonal
            - left_ratio * lower_rows(above_coef, stride, 0.0)
            - right_ratio * upper_rows(below_coef, stride, 0.0)
        )
        right_sides = (
            right_sides
            - left_ratio[None] * lower_rows(right_sides, stride, 0.0)
            - right_ratio[None] * upper_rows(right_sides, stride, 0.0)
        )
        below_coef = -left_ratio * lower_rows(below_coef, stride, 0.0)
        above_coef = -right_ratio * upper_rows(above_coef, stride, 0.0)
        stride = stride * 2
    return right_sides / diagonal[None]


def shards(phase_now, phase_old, solute, iface_blocks, iface_count):
    slab_depth, tile_width, length = phase_now.shape
    slot_total = iface_blocks.shape[-1]
    block_total = slab_depth // BZ
    own_count = iface_count.reshape(())
    block_ids = iface_blocks.reshape(slot_total)
    slot_index = jnp.arange(slot_total, dtype=jnp.int32)
    live_mask = (slot_index < own_count).astype(jnp.float32)
    widened = with_halo(jnp.stack([phase_now, solute]), (("growth", 1), ("lateral", 2)), 1)
    full_fields = jnp.pad(widened, ((0, 0), (0, 0), (0, 0), (1, 1)))
    phase_pad = full_fields[0]
    solute_pad = full_fields[1]
    grad_x = (phase_pad[1:-1, 2:, 1:-1] - phase_pad[1:-1, :-2, 1:-1]) * 0.5
    grad_y = (phase_pad[1:-1, 1:-1, 2:] - phase_pad[1:-1, 1:-1, :-2]) * 0.5
    grad_z = (phase_pad[2:, 1:-1, 1:-1] - phase_pad[:-2, 1:-1, 1:-1]) * 0.5
    features = jnp.stack([grad_x, grad_y, grad_z, phase_now - phase_old, solute])
    features = features.reshape(5, block_total, BZ, tile_width, length)
    chosen = jnp.take(features, block_ids, axis=1)
    flux_part = interface_flux(chosen)
    empty_flux = jnp.zeros((3, block_total, BZ, tile_width, length), jnp.float32)
    fluxes = empty_flux.at[:, block_ids].add(flux_part * live_mask[None, :, None, None, None])
    fluxes = fluxes.reshape(3, slab_depth, tile_width, length)
    flux_pair = with_halo(jnp.stack([fluxes[0], fluxes[2]]), (("growth", 1), ("lateral", 2)), 1)
    flux_y = jnp.pad(fluxes[1], ((0, 0), (0, 0), (1, 1)))
    source = (
        flux_pair[0, 1:-1, 2:, :]
        - flux_pair[0, 1:-1, :-2, :]
        + (flux_y[:, :, 2:] - flux_y[:, :, :-2])
        + (flux_pair[1, 2:, 1:-1, :] - flux_pair[1, :-2, 1:-1, :])
    ) * 0.5
    diff_pad = diffusivity(phase_pad)
    centre = diff_pad[1:-1, 1:-1, 1:-1]
    lateral = (centre + diff_pad[1:-1, 2:, 1:-1]) * 0.5 * (solute_pad[1:-1, 2:, 1:-1] - solute)
    lateral = lateral + (centre + diff_pad[1:-1, :-2, 1:-1]) * 0.5 * (
        solute_pad[1:-1, :-2, 1:-1] - solute
    )
    lateral = lateral + (centre + diff_pad[1:-1, 1:-1, 2:]) * 0.5 * (
        solute_pad[1:-1, 1:-1, 2:] - solute
    )
    lateral = lateral + (centre + diff_pad[1:-1, 1:-1, :-2]) * 0.5 * (
        solute_pad[1:-1, 1:-1, :-2] - solute
    )
    lateral = LATERAL_RATE * lateral
    rhs = solute + lateral + source
    lower_face = VERTICAL_RATE * (centre + diff_pad[:-2, 1:-1, 1:-1]) * 0.5
    upper_face = VERTICAL_RATE * (centre + diff_pad[2:, 1:-1, 1:-1]) * 0.5
    diagonal = 1.0 + lower_face + upper_face
    row_index = jnp.arange(slab_depth, dtype=jnp.int32)[:, None, None]
    below_coef = jnp.where(row_index == 0, 0.0, -lower_face)
    above_coef = jnp.where(row_index == slab_depth - 1, 0.0, -upper_face)
    spike_low = jnp.where(row_index == 0, lower_face, 0.0)
    spike_high = jnp.where(row_index == slab_depth - 1, upper_face, 0.0)
    spikes = local_solve(below_coef, diagonal, above_coef, jnp.stack([rhs, spike_low, spike_high]))
    boundary = jnp.stack(
        [spikes[0, 0], spikes[0, -1], spikes[1, 0], spikes[1, -1], spikes[2, 0], spikes[2, -1]]
    )
    gathered = lax.all_gather(boundary[None], "growth", axis=0, tiled=True)
    growth_total = lax.axis_size("growth")
    zero_plane = jnp.zeros((tile_width, length), jnp.float32)
    carry_u = zero_plane
    carry_f = zero_plane
    head_terms = []
    tail_terms = []
    for member in range(growth_total):
        first_p = gathered[member, 0]
        last_p = gathered[member, 1]
        first_g = gathered[member, 2]
        last_g = gathered[member, 3]
        first_h = gathered[member, 4]
        last_h = gathered[member, 5]
        pivot_value = 1.0 - first_g * carry_u
        head_f = (first_p + first_g * carry_f) / pivot_value
        head_u = first_h / pivot_value
        new_f = last_p + last_g * carry_f + last_g * carry_u * head_f
        new_u = last_g * carry_u * head_u + last_h
        carry_f = new_f
        carry_u = new_u
        head_terms.append((head_f, head_u))
        tail_terms.append((carry_f, carry_u))
    head_values = [zero_plane] * growth_total
    tail_values = [zero_plane] * growth_total
    next_head = zero_plane
    for member in reversed(range(growth_total)):
        head_values[member] = head_terms[member][0] + head_terms[member][1] * next_head
        tail_values[member] = tail_terms[member][0] + tail_terms[member][1] * next_head
        next_head = head_values[member]
    growth_index = lax.axis_index("growth")
    tail_stack = jnp.stack([zero_plane] + tail_values)
    head_stack = jnp.stack(head_values + [zero_plane])
    value_below = lax.dynamic_index_in_dim(tail_stack, growth_index, 0, keepdims=False)
    value_above = lax.dynamic_index_in_dim(head_stack, growth_index + 1, 0, keepdims=False)
    return spikes[0] + spikes[1] * value_below[None] + spikes[2] * value_above[None]


def solution(mesh):
    in_specs = (
        P("growth", "lateral", None),
        P("growth", "lateral", None),
        P("growth", "lateral", None),
        P("growth", "lateral", None),
        P("growth", "lateral"),
    )
    out_specs = P("growth", "lateral", None)
    return jax.shard_map(shards, mesh=mesh, in_specs=in_specs, out_specs=out_specs, check_vma=False)
```

profile of v0, /device:TPU:96, one launch (start us, length us, event | category | flops | bytes accessed | tf_op | source)
XLA Modules:
  0.0 81.5 jit_solution(6245446703885992582)
XLA Ops:
  0.0 0.9 %pad_maximum_fusion.24 = (f32[2,1,32,128]{3,2,1,0:T(8,128)S(1)}, f32[2,1,32,128]{3,2,1,0:T(8,128)S(1)}) fusion(f32[1,32,32,128]{3,2,1,0:T(8,128)} %bitcast.297, f32[1,32,32,128]{3,2,1,0:T(8,128)} %bitcast.301), kind=kLoop, calls=%fused_computation.164 | loop fusion | flops 16384 | bytes 1114112 | tf_op jit(solution)/shard_map/slice | solution.py:24
  0.9 1.4 %collective-permute-start.1 = (f32[2,1,32,128]{3,2,1,0:T(8,128)S(1)}, f32[2,1,32,128]{3,2,1,0:T(8,128)S(1)}, u32[]{:S(2)}, u32[]{:S(2)}) collective-permute-start(f32[2,1,32,128]{3,2,1,0:T(8,128)S(1)} %get-tuple-element.69), channel_id=1, source_target_pairs={{32,0},{64,32},{96,64},{33,1},{65,33},{97,65},{34,2},{66,34},{98,6... | collective-permute-start | bytes 98312 | tf_op jit(solution)/shard_map/ppermute | solution.py:29
  2.3 4.5 %collective-permute-start = (f32[2,1,32,128]{3,2,1,0:T(8,128)S(1)}, f32[2,1,32,128]{3,2,1,0:T(8,128)S(1)}, u32[]{:S(2)}, u32[]{:S(2)}) collective-permute-start(f32[2,1,32,128]{3,2,1,0:T(8,128)S(1)} %get-tuple-element.68), channel_id=1, source_target_pairs={{0,32},{32,64},{64,96},{1,33},{33,65},{65,97},{2,34},{34,66},{66,9... | collective-permute-start | bytes 98312 | tf_op jit(solution)/shard_map/ppermute | solution.py:27
  9.5 1.2 %pad_maximum_fusion.20 = (f32[2,34,1,128]{3,2,1,0:T(1,128)S(1)}, f32[2,34,1,128]{3,2,1,0:T(1,128)S(1)}) fusion(f32[2,1,32,128]{3,2,1,0:T(8,128)S(1)} %collective-permute-done.1, f32[2,1,32,128]{3,2,1,0:T(8,128)S(1)} %collective-permute-done, f32[1,32,32,128]{3,2,1,0:T(8,128)} %bitcast.298, f32[1,32,32,128]{3,2,1,0:T(8,128)} %bitcast.302), kind=kLoop, calls=%fused_computation.160 | loop fusion | flops 52224 | bytes 1183744 | tf_op jit(solution)/shard_map/slice | solution.py:24
  10.6 3.6 %collective-permute-start.3 = (f32[2,34,1,128]{3,2,1,0:T(1,128)S(1)}, f32[2,34,1,128]{3,2,1,0:T(1,128)S(1)}, u32[]{:S(2)}, u32[]{:S(2)}) collective-permute-start(f32[2,34,1,128]{3,2,1,0:T(1,128)S(1)} %get-tuple-element.65), channel_id=1, source_target_pairs={{1,0},{2,1},{3,2},{4,3},{5,4},{6,5},{7,6},{8,7},{9,8},{10,9},{11,1... | collective-permute-start | bytes 104456 | tf_op jit(solution)/shard_map/ppermute | solution.py:29
  14.3 1.9 %collective-permute-start.2 = (f32[2,34,1,128]{3,2,1,0:T(1,128)S(1)}, f32[2,34,1,128]{3,2,1,0:T(1,128)S(1)}, u32[]{:S(2)}, u32[]{:S(2)}) collective-permute-start(f32[2,34,1,128]{3,2,1,0:T(1,128)S(1)} %get-tuple-element.64), channel_id=1, source_target_pairs={{0,1},{1,2},{2,3},{3,4},{4,5},{5,6},{6,7},{7,8},{8,9},{9,10},{10,1... | collective-permute-start | bytes 104456 | tf_op jit(solution)/shard_map/ppermute | solution.py:27
  16.4 5.3 %collective-permute-done.2 = f32[2,34,1,128]{3,2,1,0:T(1,128)S(1)} collective-permute-done((f32[2,34,1,128]{3,2,1,0:T(1,128)S(1)}, f32[2,34,1,128]{3,2,1,0:T(1,128)S(1)}, u32[]{:S(2)}, u32[]{:S(2)}) %collective-permute-start.2) | collective-permute-done | bytes 34848 | tf_op jit(solution)/shard_map/ppermute | solution.py:27
  21.7 2.5 %select_maximum_fusion = f32[2,34,34,130]{3,2,1,0:T(8,128)S(1)} fusion(f32[2,34,1,128]{3,2,1,0:T(1,128)S(1)} %collective-permute-done.3, f32[2,34,1,128]{3,2,1,0:T(1,128)S(1)} %collective-permute-done.2, f32[2,1,32,128]{3,2,1,0:T(8,128)S(1)} %collective-permute-done.1, f32[2,1,32,128]{3,2,1,0:T(8,128)S(1)} %collective-permute-done, ...), kind=kLoop, calls=%fused_computation.4 | loop fusion | flops 4207840 | bytes 2385984 | tf_op jit(solution)/shard_map/concatenate | solution.py:25
  24.4 1.4 %slice_bitcast_fusion = (f32[34,34,130]{2,1,0:T(8,128)}, f32[34,34,130]{2,1,0:T(8,128)S(1)}) fusion(f32[2,34,34,130]{3,2,1,0:T(8,128)S(1)} %select_maximum_fusion), kind=kLoop, calls=%fused_computation.17 | loop fusion | bytes 2404480 | tf_op jit(solution)/shard_map/squeeze | solution.py:108
  27.3 0.9 %constant_dynamic-update-slice_fusion.3 = f32[5,8,4,32,128]{4,3,2,1,0:T(8,128)} fusion(f32[5,8,4,32,128]{4,3,2,1,0:T(8,128)} %constant_dynamic-update-slice_fusion.4, f32[1,8,4,32,128]{4,3,2,1,0:T(8,128)S(1)} %bitcast.312), kind=kLoop, calls=%fused_computation.135 | loop fusion | bytes 1048576
  28.2 0.9 %constant_dynamic-update-slice_fusion.2 = f32[5,8,4,32,128]{4,3,2,1,0:T(8,128)} fusion(f32[5,8,4,32,128]{4,3,2,1,0:T(8,128)} %constant_dynamic-update-slice_fusion.3, f32[1,8,4,32,128]{4,3,2,1,0:T(8,128)S(1)} %bitcast.311), kind=kLoop, calls=%fused_computation.134 | loop fusion | bytes 1048576
  29.0 0.9 %constant_dynamic-update-slice_fusion.1 = f32[5,8,4,32,128]{4,3,2,1,0:T(8,128)} fusion(f32[5,8,4,32,128]{4,3,2,1,0:T(8,128)} %constant_dynamic-update-slice_fusion.2, f32[1,8,4,32,128]{4,3,2,1,0:T(8,128)S(1)} %bitcast.310), kind=kLoop, calls=%fused_computation.133 | loop fusion | bytes 1048576
  30.7 3.7 %gather_fusion = f32[6,5,4,32,128]{4,3,2,1,0:T(8,128)} fusion(f32[5,8,4,32,128]{4,3,2,1,0:T(8,128)} %constant_dynamic-update-slice_fusion, s32[1024]{0:T(1024)S(1)} %pad_clamp_fusion), kind=kCustom, calls=%fused_computation | custom fusion | bytes 3932184 | tf_op jit(solution)/shard_map/jit(_take)/gather | solution.py:114
  34.4 1.8 %select_bitcast_fusion = f32[5,6,4,32,128]{4,3,2,0,1:T(8,128)S(1)} fusion(f32[6,5,4,32,128]{4,3,2,1,0:T(8,128)} %gather_fusion, pred[6]{0:T(512)(128)(4,1)S(1)} %compare_and_fusion), kind=kLoop, calls=%fused_computation.10 | loop fusion | flops 491520 | bytes 3932166 | tf_op jit(solution)/shard_map/jit(_take)/select_n | solution.py:114
  36.8 1.3 %fusion.1 = f32[6,3,4,32,128]{4,3,2,1,0:T(8,128)} fusion(f32[1,6,4,32,128]{4,3,2,0,1:T(8,128)S(1)} %get-tuple-element.38, f32[1,6,4,32,128]{4,3,2,0,1:T(8,128)S(1)} %get-tuple-element.37, f32[1,6,4,32,128]{4,3,2,0,1:T(8,128)S(1)} %get-tuple-element.33, f32[6]{0:T(128)S(1)} %compare_convert_fusion), kind=kLoop, calls=%fused_computation.23 | loop fusion | flops 884736 | bytes 2359320 | tf_op jit(solution)/shard_map/mul | solution.py:117
  38.3 2.6 %scatter_fusion = f32[3,8,4,32,128]{4,3,2,1,0:T(8,128)S(1)} fusion(f32[3,8,4,32,128]{4,3,2,1,0:T(8,128)S(1)} %broadcast_in_dim.67, s32[6]{0:T(128)S(1)} %fusion.73, f32[6,3,4,32,128]{4,3,2,1,0:T(8,128)} %fusion.1), kind=kCustom, calls=%fused_computation.1 | custom fusion | flops 294912 | bytes 3538968 | tf_op jit(solution)/shard_map/scatter-add | solution.py:117
  41.1 3.4 %collective-permute-start.4 = (f32[2,1,32,128]{3,2,1,0:T(8,128)S(1)}, f32[2,1,32,128]{3,2,1,0:T(8,128)S(1)}, u32[]{:S(2)}, u32[]{:S(2)}) collective-permute-start(f32[2,1,32,128]{3,2,1,0:T(8,128)S(1)} %get-tuple-element.67), channel_id=1, source_target_pairs={{0,32},{32,64},{64,96},{1,33},{33,65},{65,97},{2,34},{34,66},{66,9... | collective-permute-start | bytes 98312 | tf_op jit(solution)/shard_map/ppermute | solution.py:27
  44.5 1.3 %collective-permute-start.5 = (f32[2,1,32,128]{3,2,1,0:T(8,128)S(1)}, f32[2,1,32,128]{3,2,1,0:T(8,128)S(1)}, u32[]{:S(2)}, u32[]{:S(2)}) collective-permute-start(f32[2,1,32,128]{3,2,1,0:T(8,128)S(1)} %get-tuple-element.66), channel_id=1, source_target_pairs={{32,0},{64,32},{96,64},{33,1},{65,33},{97,65},{34,2},{66,34},{98,6... | collective-permute-start | bytes 98312 | tf_op jit(solution)/shard_map/ppermute | solution.py:29
  50.3 1.9 %collective-permute-start.7 = (f32[2,34,1,128]{3,2,1,0:T(1,128)S(1)}, f32[2,34,1,128]{3,2,1,0:T(1,128)S(1)}, u32[]{:S(2)}, u32[]{:S(2)}) collective-permute-start(f32[2,34,1,128]{3,2,1,0:T(1,128)S(1)} %get-tuple-element.63), channel_id=1, source_target_pairs={{0,1},{1,2},{2,3},{3,4},{4,5},{5,6},{6,7},{7,8},{8,9},{9,10},{10,1... | collective-permute-start | bytes 104456 | tf_op jit(solution)/shard_map/ppermute | solution.py:27
  52.3 5.9 %collective-permute-start.6 = (f32[2,34,1,128]{3,2,1,0:T(1,128)S(1)}, f32[2,34,1,128]{3,2,1,0:T(1,128)S(1)}, u32[]{:S(2)}, u32[]{:S(2)}) collective-permute-start(f32[2,34,1,128]{3,2,1,0:T(1,128)S(1)} %get-tuple-element.62), channel_id=1, source_target_pairs={{1,0},{2,1},{3,2},{4,3},{5,4},{6,5},{7,6},{8,7},{9,8},{10,9},{11,1... | collective-permute-start | bytes 104456 | tf_op jit(solution)/shard_map/ppermute | solution.py:29
  58.5 1.1 %collective-permute-done.6 = f32[2,34,1,128]{3,2,1,0:T(1,128)S(1)} collective-permute-done((f32[2,34,1,128]{3,2,1,0:T(1,128)S(1)}, f32[2,34,1,128]{3,2,1,0:T(1,128)S(1)}, u32[]{:S(2)}, u32[]{:S(2)}) %collective-permute-start.6) | collective-permute-done | bytes 34848 | tf_op jit(solution)/shard_map/ppermute | solution.py:29
  59.6 1.4 %fusion.7 = f32[1,32,32,128]{3,2,1,0:T(8,128)S(1)} fusion(f32[32,32,128]{2,1,0:T(8,128)S(1)} %bitcast.314, f32[2,1,32,128]{3,2,1,0:T(8,128)S(1)} %collective-permute-done.4, f32[1,32,32,128]{3,2,1,0:T(8,128)S(1)} %bitcast.309, f32[1,32,32,128]{3,2,1,0:T(8,128)S(1)} %bitcast.306, f32[2,1,32,128]{3,2,1,0:T(8,128)S(1)} %collective-permute-done.5, ...), kind=kLoop, calls=%fused_computation.34 | loop fusion | flops 5242880 | bytes 7475200 | tf_op jit(solution)/shard_map/stack | solution.py:149
  66.2 14.1 %all-gather = f32[24,32,128]{2,1,0:T(8,128)S(1)} all-gather(f32[6,32,128]{2,1,0:T(8,128)S(1)} %constant_dynamic-update-slice_fusion.5), channel_id=2, replica_groups=mesh['growth'=4,'lateral'=32] {'growth'}, dimensions={0}, use_global_device_ids=true | all-gather | bytes 491520 | tf_op jit(solution)/shard_map/all_gather | solution.py:153
  80.5 1.0 %fusion.9 = f32[32,32,128]{2,1,0:T(8,128)} fusion(f32[3,32,32,128]{3,2,1,0:T(8,128)S(1)} %subtract_divide_fusion, f32[32,128]{1,0:T(8,128)S(1)} %dynamic-slice_bitcast_fusion, f32[32,128]{1,0:T(8,128)S(1)} %dynamic-slice_bitcast_fusion.1), kind=kLoop, calls=%fused_computation.37 | loop fusion | flops 524288 | bytes 2129920 | tf_op jit(solution)/shard_map/add | solution.py:188
  (90 shorter events, 15.4 us)
Async XLA Ops:
  0.0 16.2 %copy-start.2 = (f32[32,32,128]{2,1,0:T(8,128)S(1)}, f32[32,32,128]{2,1,0:T(8,128)}, u32[]{:S(2)}) copy-start(f32[32,32,128]{2,1,0:T(8,128)} %param.5) | copy-start | bytes 1572868
  0.0 16.2 %copy-start.3 = (f32[32,32,128]{2,1,0:T(8,128)S(1)}, f32[32,32,128]{2,1,0:T(8,128)}, u32[]{:S(2)}) copy-start(f32[32,32,128]{2,1,0:T(8,128)} %param.6) | copy-start | bytes 1572868
  0.9 20.8 %copy-start = (f32[32,32,128]{2,1,0:T(8,128)S(1)}, f32[32,32,128]{2,1,0:T(8,128)}, u32[]{:S(2)}) copy-start(f32[32,32,128]{2,1,0:T(8,128)} %param.7) | copy-start | bytes 1572868
  0.9 8.6 %collective-permute-start.1 = (f32[2,1,32,128]{3,2,1,0:T(8,128)S(1)}, f32[2,1,32,128]{3,2,1,0:T(8,128)S(1)}, u32[]{:S(2)}, u32[]{:S(2)}) collective-permute-start(f32[2,1,32,128]{3,2,1,0:T(8,128)S(1)} %get-tuple-element.69), channel_id=1, source_target_pairs={{32,0},{64,32},{96,64},{33,1},{65,33},{97,65},{34,2},{66,34},{98,6... | collective-permute-start | bytes 98312 | tf_op jit(solution)/shard_map/ppermute | solution.py:29
  2.3 7.2 %collective-permute-start = (f32[2,1,32,128]{3,2,1,0:T(8,128)S(1)}, f32[2,1,32,128]{3,2,1,0:T(8,128)S(1)}, u32[]{:S(2)}, u32[]{:S(2)}) collective-permute-start(f32[2,1,32,128]{3,2,1,0:T(8,128)S(1)} %get-tuple-element.68), channel_id=1, source_target_pairs={{0,32},{32,64},{64,96},{1,33},{33,65},{65,97},{2,34},{34,66},{66,9... | collective-permute-start | bytes 98312 | tf_op jit(solution)/shard_map/ppermute | solution.py:27
  10.6 5.7 %collective-permute-start.3 = (f32[2,34,1,128]{3,2,1,0:T(1,128)S(1)}, f32[2,34,1,128]{3,2,1,0:T(1,128)S(1)}, u32[]{:S(2)}, u32[]{:S(2)}) collective-permute-start(f32[2,34,1,128]{3,2,1,0:T(1,128)S(1)} %get-tuple-element.65), channel_id=1, source_target_pairs={{1,0},{2,1},{3,2},{4,3},{5,4},{6,5},{7,6},{8,7},{9,8},{10,9},{11,1... | collective-permute-start | bytes 104456 | tf_op jit(solution)/shard_map/ppermute | solution.py:29
  14.3 7.4 %collective-permute-start.2 = (f32[2,34,1,128]{3,2,1,0:T(1,128)S(1)}, f32[2,34,1,128]{3,2,1,0:T(1,128)S(1)}, u32[]{:S(2)}, u32[]{:S(2)}) collective-permute-start(f32[2,34,1,128]{3,2,1,0:T(1,128)S(1)} %get-tuple-element.64), channel_id=1, source_target_pairs={{0,1},{1,2},{2,3},{3,4},{4,5},{5,6},{6,7},{7,8},{8,9},{9,10},{10,1... | collective-permute-start | bytes 104456 | tf_op jit(solution)/shard_map/ppermute | solution.py:27
  41.1 9.1 %collective-permute-start.4 = (f32[2,1,32,128]{3,2,1,0:T(8,128)S(1)}, f32[2,1,32,128]{3,2,1,0:T(8,128)S(1)}, u32[]{:S(2)}, u32[]{:S(2)}) collective-permute-start(f32[2,1,32,128]{3,2,1,0:T(8,128)S(1)} %get-tuple-element.67), channel_id=1, source_target_pairs={{0,32},{32,64},{64,96},{1,33},{33,65},{65,97},{2,34},{34,66},{66,9... | collective-permute-start | bytes 98312 | tf_op jit(solution)/shard_map/ppermute | solution.py:27
  44.5 5.8 %collective-permute-start.5 = (f32[2,1,32,128]{3,2,1,0:T(8,128)S(1)}, f32[2,1,32,128]{3,2,1,0:T(8,128)S(1)}, u32[]{:S(2)}, u32[]{:S(2)}) collective-permute-start(f32[2,1,32,128]{3,2,1,0:T(8,128)S(1)} %get-tuple-element.66), channel_id=1, source_target_pairs={{32,0},{64,32},{96,64},{33,1},{65,33},{97,65},{34,2},{66,34},{98,6... | collective-permute-start | bytes 98312 | tf_op jit(solution)/shard_map/ppermute | solution.py:29
  50.3 8.2 %collective-permute-start.7 = (f32[2,34,1,128]{3,2,1,0:T(1,128)S(1)}, f32[2,34,1,128]{3,2,1,0:T(1,128)S(1)}, u32[]{:S(2)}, u32[]{:S(2)}) collective-permute-start(f32[2,34,1,128]{3,2,1,0:T(1,128)S(1)} %get-tuple-element.63), channel_id=1, source_target_pairs={{0,1},{1,2},{2,3},{3,4},{4,5},{5,6},{6,7},{7,8},{8,9},{9,10},{10,1... | collective-permute-start | bytes 104456 | tf_op jit(solution)/shard_map/ppermute | solution.py:27
  52.3 7.4 %collective-permute-start.6 = (f32[2,34,1,128]{3,2,1,0:T(1,128)S(1)}, f32[2,34,1,128]{3,2,1,0:T(1,128)S(1)}, u32[]{:S(2)}, u32[]{:S(2)}) collective-permute-start(f32[2,34,1,128]{3,2,1,0:T(1,128)S(1)} %get-tuple-element.62), channel_id=1, source_target_pairs={{1,0},{2,1},{3,2},{4,3},{5,4},{6,5},{7,6},{8,7},{9,8},{10,9},{11,1... | collective-permute-start | bytes 104456 | tf_op jit(solution)/shard_map/ppermute | solution.py:29
  58.2 1.4 %copy-start.1 = (f32[34,34,130]{2,1,0:T(8,128)S(1)}, f32[34,34,130]{2,1,0:T(8,128)}, u32[]{:S(2)}) copy-start(f32[34,34,130]{2,1,0:T(8,128)} %get-tuple-element.35) | copy-start | bytes 1803364
  65.5 14.8 %copy-start.4 = (f32[5,32,128]{2,1,0:T(8,128)S(1)}, f32[5,32,128]{2,1,0:T(8,128)}, u32[]{:S(2)}) copy-start(f32[5,32,128]{2,1,0:T(8,128)} %constant_dynamic-update-slice_fusion.15) | copy-start | bytes 245764
where the time goes:
time: 82 us; the launch traced here: 81.5 us
  starting transfers between devices  24.1 us (29%)
  other arithmetic  22.1 us (27%)
  blocking collectives  14.1 us (17%)
  local copies, waits for them, and re-layouts  13.4 us (16%)
  waiting for transfers between devices  6.46 us (8%)
  between operations  1.35 us (2%)
    all_gather x1, blocking collectives, shards(): gathered = lax.all_gather(boundary[None], 'growth', axis=0, tiled=True)  14.1 us
    ppermute x4, starting transfers between devices, with_halo(): lax.ppermute(head, axis, [((i + 1) % count, i) for i in range(ends)])  12.3 us
    ppermute x4, starting transfers between devices, with_halo(): lax.ppermute(tail, axis, [(i, (i + 1) % count) for i in range(ends)])  11.8 us
    ppermute x4, waiting for transfers between devices, with_halo(): lax.ppermute(tail, axis, [(i, (i + 1) % count) for i in range(ends)])  5.31 us
    unnamed x22, local copies, waits for them, and re-layouts  4.07 us
    gather x1, local copies, waits for them, and re-layouts, shards(): chosen = jnp.take(features, block_ids, axis=1)  3.71 us
    scatter-add x1, other arithmetic, shards(): empty_flux.at[:, block_ids]  2.63 us
    sub x4, other arithmetic, local_solve(): right_sides - left_ratio[None] * lower_rows(right_sides, stride, 0.0)  2.62 us
  transfers between devices with their start and end apart: 8, of which 3 were waited for; matrix products, arithmetic and copies ran while one was open for 8% of the time, Pallas kernels for 0%

commit v1 on v0

v1 whole, which is shorter than its diff:
```python
import jax
import jax.numpy as jnp
from jax import lax
from jax.experimental import pallas as pl
from jax.experimental.pallas import tpu as pltpu
from jax.sharding import PartitionSpec as P

BZ = 4
MESH = pl.DeviceIdType.MESH
NG = 4
NL = 32
CZ = 32
CX = 32
NY = 128
PAD = 8
ROW = CX + 2 * PAD
F32 = jnp.float32


def flux_factor(gx, gy, gz, pre):
    x2 = gx * gx
    y2 = gy * gy
    z2 = gz * gz
    inv = lax.rsqrt(x2 + y2 + z2 + 1.0)
    inv2 = inv * inv
    quartic = x2 * x2 + y2 * y2 + z2 * z2
    return pre * inv * (0.1 + 1.2 * quartic * (inv2 * inv2))


def next_y(a, last):
    return jnp.where(last, 0.0, pltpu.roll(a, NY - 1, 1))


def prev_y(a, first):
    return jnp.where(first, 0.0, pltpu.roll(a, 1, 1))


def kernel(
    phase, old, solute, blocks, count, out,
    ph, so, po, s0, fx, fz, rh, ee, wf, pf, vb, dd, pp, qq, col,
    xs, xr, zs, zr, cs, cr, sts, str_, pvs, pvr, blk, cnt,
    in_sem, x_ss, x_rs, z_ss, z_rs, c_ss, c_rs, st_ss, st_rs, pv_ss, pv_rs,
):
    g = lax.axis_index("growth")
    l = lax.axis_index("lateral")
    has_lo, has_hi = g > 0, g < NG - 1
    has_xl, has_xr = l > 0, l < NL - 1
    g_lo, g_hi = jnp.maximum(g - 1, 0), jnp.minimum(g + 1, NG - 1)
    l_lo, l_hi = jnp.maximum(l - 1, 0), jnp.minimum(l + 1, NL - 1)
    others = [lax.rem(g + d, NG) for d in range(1, NG)]

    barrier = pltpu.get_barrier_semaphore()

    def greet(cond, dev):
        @pl.when(cond)
        def _():
            pl.semaphore_signal(barrier, inc=1, device_id=dev, device_id_type=MESH)

    diag = [
        (has_lo & has_xl, (g_lo, l_lo)),
        (has_lo & has_xr, (g_lo, l_hi)),
        (has_hi & has_xl, (g_hi, l_lo)),
        (has_hi & has_xr, (g_hi, l_hi)),
    ]
    greet(has_xl, (g, l_lo))
    greet(has_xr, (g, l_hi))
    for cond, dev in diag:
        greet(cond, dev)
    for o in others:
        pl.semaphore_signal(barrier, inc=1, device_id=(o, l), device_id_type=MESH)

    ins = [
        pltpu.make_async_copy(phase, ph.at[pl.ds(1, CZ), pl.ds(PAD, CX), :], in_sem.at[0]),
        pltpu.make_async_copy(old, po, in_sem.at[1]),
        pltpu.make_async_copy(solute, so.at[:, pl.ds(PAD, CX), :], in_sem.at[2]),
        pltpu.make_async_copy(blocks, blk, in_sem.at[3]),
        pltpu.make_async_copy(count, cnt, in_sem.at[4]),
    ]
    for c in ins:
        c.start()

    lane = lax.broadcasted_iota(jnp.int32, (CX, NY), 1)
    first, last = lane == 0, lane == NY - 1
    zero = jnp.zeros((CX, NY), F32)

    def face(a, b):
        return 220.0 - 90.0 * (a + b)

    def phz(z, off=0):
        return ph[z + 1, pl.ds(PAD + off, CX), :]

    def soz(z, off=0):
        return so[z, pl.ds(PAD + off, CX), :]

    ins[0].wait()
    bottom = jnp.where(g == 0, face(phz(0), 0.0), zero) + 1.0
    top = jnp.where(g == NG - 1, face(phz(CZ - 1), 0.0), zero) + 1.0
    ee[0] = bottom
    pf[0] = zero + 1.0

    def up(i, carry):
        e, prod = carry
        u = face(phz(i), phz(i + 1))
        w = u / (u + e)
        e = 1.0 + w * e
        prod = prod * w
        wf[i] = w
        ee[i + 1] = e
        pf[i + 1] = prod
        return e, prod

    e_top, prod_top = lax.fori_loop(0, CZ - 1, up, (bottom, zero + 1.0))

    def finish(i, e, prod):
        d = 1.0 / (ee[i] + e - 1.0)
        dd[i] = d
        pp[i] = pf[i] * d
        qq[i] = prod * d

    def down(j, carry):
        i = CZ - 1 - j
        e, prod = carry
        finish(i, e, prod)
        u = face(phz(i), phz(i - 1))
        v = u / (u + e)
        vb[i] = v
        return 1.0 + v * e, prod * v

    e_bot, prod_bot = lax.fori_loop(0, CZ - 1, down, (top, zero + 1.0))
    finish(0, e_bot, prod_bot)

    for c in ins[1:]:
        c.wait()

    def prefactor(k, _):
        hit = jnp.int32(0)
        for s in range(6):
            hit = hit | jnp.where((blk[0, 0, s] == k) & (s < cnt[0, 0]), 1, 0)
        mask = hit.astype(F32) * 0.25
        for r in range(BZ):
            z = k * BZ + r
            s0[z] = (1.0 + 0.7 * soz(z)) * (phz(z) - po[z]) * mask
        return 0

    lax.fori_loop(0, CZ // BZ, prefactor, 0)

    for side, x in ((0, 0), (1, CX - 1)):
        inner = 1 if x == 0 else CX - 2
        xs[side, 0] = ph[1:CZ + 1, PAD + x, :]
        xs[side, 1] = ph[1:CZ + 1, PAD + inner, :]
        xs[side, 2] = so[:, PAD + x, :]
        xs[side, 3] = s0[:, x, :]
    for side, z in ((0, 0), (1, CZ - 1)):
        zs[side, 0] = phz(z)
        zs[side, 1] = phz(1 if z == 0 else CZ - 2)
        zs[side, 2] = s0[z]
        zs[side, 3] = pp[0] if z == 0 else qq[CZ - 1]
        cs[2 * side] = phz(z)[0:8]
        cs[2 * side + 1] = phz(z)[CX - 8:CX]

    pl.semaphore_wait(
        barrier,
        NG - 1
        + has_xl.astype(jnp.int32) * (1 + has_lo.astype(jnp.int32) + has_hi.astype(jnp.int32))
        + has_xr.astype(jnp.int32) * (1 + has_lo.astype(jnp.int32) + has_hi.astype(jnp.int32)),
    )

    def remote(src, dst, ss, rs, dev):
        return pltpu.make_async_remote_copy(
            src_ref=src, dst_ref=dst, send_sem=ss, recv_sem=rs, device_id=dev, device_id_type=MESH
        )

    x_out = [
        (has_xl, remote(xs.at[0], xr.at[1], x_ss.at[0], x_rs.at[1], (g, l_lo))),
        (has_xr, remote(xs.at[1], xr.at[0], x_ss.at[1], x_rs.at[0], (g, l_hi))),
    ]
    z_out = [
        (has_lo, remote(zs.at[0], zr.at[1], z_ss.at[0], z_rs.at[1], (g_lo, l))),
        (has_hi, remote(zs.at[1], zr.at[0], z_ss.at[1], z_rs.at[0], (g_hi, l))),
    ]
    c_out = [
        (cond, remote(cs.at[i], cr.at[3 - i], c_ss.at[i], c_rs.at[3 - i], dev))
        for i, (cond, dev) in enumerate(diag)
    ]
    for cond, cp in x_out + c_out + z_out:
        pl.when(cond)(cp.start)

    x_in = [
        (has_xl, remote(xs.at[1], xr.at[0], x_ss.at[1], x_rs.at[0], (g, l_lo))),
        (has_xr, remote(xs.at[0], xr.at[1], x_ss.at[0], x_rs.at[1], (g, l_hi))),
    ]
    z_in = [
        (has_lo, remote(zs.at[1], zr.at[0], z_ss.at[1], z_rs.at[0], (g_lo, l))),
        (has_hi, remote(zs.at[0], zr.at[1], z_ss.at[0], z_rs.at[1], (g_hi, l))),
    ]
    c_in = [
        (cond, remote(cs.at[3 - i], cr.at[i], c_ss.at[3 - i], c_rs.at[i], dev))
        for i, (cond, dev) in enumerate(diag)
    ]

    for side, here in ((0, has_xl), (1, has_xr)):
        @pl.when(jnp.logical_not(here))
        def _():
            xr[side] = jnp.zeros((4, CZ, NY), F32)
    for side, here in ((0, has_lo), (1, has_hi)):
        @pl.when(jnp.logical_not(here))
        def _():
            zr[side] = jnp.zeros((4, CX, NY), F32)
    for i, (cond, _) in enumerate(diag):
        @pl.when(jnp.logical_not(cond))
        def _():
            cr[i] = jnp.zeros((8, NY), F32)

    for cond, cp in z_in:
        pl.when(cond)(cp.wait_recv)
    sts[0] = 1.0 / face(phz(CZ - 1), zr[1, 0]) + qq[CZ - 1] + zr[1, 3]
    sts[1] = pp[CZ - 1]
    str_[g] = sts[...]

    st_out = [remote(sts, str_.at[g], st_ss.at[d], st_rs.at[g], (o, l)) for d, o in enumerate(others)]
    for cp in st_out:
        cp.start()

    for cond, cp in x_in + c_in:
        pl.when(cond)(cp.wait_recv)

    ph[0, pl.ds(PAD, CX), :] = zr[0, 0]
    ph[CZ + 1, pl.ds(PAD, CX), :] = zr[1, 0]
    for side, x in ((0, -1), (1, CX)):
        ph[1:CZ + 1, PAD + x, :] = xr[side, 0]
        so[:, PAD + x, :] = xr[side, 2]
        row_lo = cr[side][7:8] if side == 0 else cr[side][0:1]
        row_hi = cr[2 + side][7:8] if side == 0 else cr[2 + side][0:1]
        ph[0, PAD + x:PAD + x + 1, :] = row_lo
        ph[CZ + 1, PAD + x:PAD + x + 1, :] = row_hi
        col[side, 7:8, :] = row_lo
        col[side, 8:40, :] = xr[side, 0]
        col[side, 40:41, :] = row_hi

    def ydiff(a):
        return next_y(a, last) - prev_y(a, first)

    for side, x in ((0, -1), (1, CX)):
        here = xr[side, 0]
        if side == 0:
            gx = ph[1:CZ + 1, PAD, :] - xr[side, 1]
        else:
            gx = xr[side, 1] - ph[1:CZ + 1, PAD + CX - 1, :]
        gz = col[side, 9:41, :] - col[side, 7:39, :]
        fx[:, PAD + x, :] = flux_factor(gx, ydiff(here), gz, xr[side, 3]) * gx
    for side, z in ((0, -1), (1, CZ)):
        here = zr[side, 0]
        gz = phz(0) - zr[side, 1] if side == 0 else zr[side, 1] - phz(CZ - 1)
        gx = phz(z, 1) - phz(z, -1)
        fz[z + 1] = flux_factor(gx, ydiff(here), gz, zr[side, 2]) * gz

    def coupling(a, b):
        return 0.055 - 0.0225 * (a + b)

    def cells(k, _):
        for r in range(BZ):
            z = k * BZ + r
            here = phz(z)
            right, left = phz(z, 1), phz(z, -1)
            yn, yp = next_y(here, last), prev_y(here, first)
            gx = right - left
            gy = yn - yp
            gz = phz(z + 1) - phz(z - 1)
            factor = flux_factor(gx, gy, gz, s0[z])
            fx[z, pl.ds(PAD, CX), :] = factor * gx
            fz[z + 1] = factor * gz
            flux_y = factor * gy
            s = soz(z)
            side = coupling(here, right) * (soz(z, 1) - s) + coupling(here, left) * (soz(z, -1) - s)
            side = side + coupling(here, yn) * (next_y(s, last) - s)
            side = side + coupling(here, yp) * (prev_y(s, first) - s)
            rh[z] = s + side + ydiff(flux_y)
        return 0

    lax.fori_loop(0, CZ // BZ, cells, 0)

    def rhs(k, _):
        for r in range(BZ):
            z = k * BZ + r
            rh[z] = (
                rh[z]
                + (fx[z, pl.ds(PAD + 1, CX), :] - fx[z, pl.ds(PAD - 1, CX), :])
                + (fz[z + 2] - fz[z])
            )
        return 0

    lax.fori_loop(0, CZ // BZ, rhs, 0)

    ee[0] = rh[0]

    def sweep_up(i, f):
        f = rh[i] + wf[i - 1] * f
        ee[i] = f
        return f

    f_top = lax.fori_loop(1, CZ, sweep_up, rh[0])

    def sweep_down(j, b):
        i = CZ - 1 - j
        r = rh[i]
        b = b + r
        ee[i] = (ee[i] + b - r) * dd[i]
        return b * vb[i]

    b_bot = lax.fori_loop(0, CZ - 1, sweep_down, zero) + rh[0]
    ee[0] = b_bot * dd[0]

    pvs[0] = ee[0]
    pvs[1] = ee[CZ - 1]
    pvr[g] = pvs[...]
    pv_out = [remote(pvs, pvr.at[g], pv_ss.at[d], pv_rs.at[g], (o, l)) for d, o in enumerate(others)]
    for cp in pv_out:
        cp.start()

    def arrive(src, dst, ss, rs):
        for o in others:
            remote(src, dst.at[o], ss.at[0], rs.at[o], (o, l)).wait_recv()

    arrive(sts, str_, st_ss, st_rs)
    m0 = 1.0 / str_[0, 0]
    t1, t2 = str_[1, 1], str_[2, 1]
    k1 = t1 * m0
    m1 = 1.0 / (str_[1, 0] - t1 * k1)
    k2 = t2 * m1
    m2 = 1.0 / (str_[2, 0] - t2 * k2)
    arrive(pvs, pvr, pv_ss, pv_rs)
    b0 = pvr[0, 1] - pvr[1, 0]
    b1 = pvr[1, 1] - pvr[2, 0] + k1 * b0
    b2 = pvr[2, 1] - pvr[3, 0] + k2 * b1
    q2 = b2 * m2
    q1 = b1 * m1 + k2 * q2
    q0 = b0 * m0 + k1 * q1
    below = jnp.where(g == 1, q0, jnp.where(g == 2, q1, jnp.where(g == 3, q2, 0.0)))
    above = jnp.where(g == 0, q0, jnp.where(g == 1, q1, jnp.where(g == 2, q2, 0.0)))

    def close(k, _):
        for r in range(BZ):
            z = k * BZ + r
            out[z] = ee[z] + pp[z] * below - qq[z] * above
        return 0

    lax.fori_loop(0, CZ // BZ, close, 0)

    for cond, cp in x_out + z_out + c_out:
        pl.when(cond)(cp.wait_send)
    for cp in st_out + pv_out:
        cp.wait_send()


def step(phase, old, solute, blocks, count):
    slab = pltpu.VMEM((CZ, CX, NY), F32)
    dma = pltpu.SemaphoreType.DMA
    return pl.pallas_call(
        kernel,
        out_shape=jax.ShapeDtypeStruct((CZ, CX, NY), F32),
        in_specs=[pl.BlockSpec(memory_space=pl.ANY)] * 5,
        out_specs=pl.BlockSpec(memory_space=pltpu.VMEM),
        scratch_shapes=[
            pltpu.VMEM((CZ + 2, ROW, NY), F32),
            pltpu.VMEM((CZ, ROW, NY), F32),
            slab,
            slab,
            pltpu.VMEM((CZ, ROW, NY), F32),
            pltpu.VMEM((CZ + 2, CX, NY), F32),
            slab, slab, slab, slab, slab, slab, slab, slab,
            pltpu.VMEM((2, ROW, NY), F32),
            pltpu.VMEM((2, 4, CZ, NY), F32),
            pltpu.VMEM((2, 4, CZ, NY), F32),
            pltpu.VMEM((2, 4, CX, NY), F32),
            pltpu.VMEM((2, 4, CX, NY), F32),
            pltpu.VMEM((4, 8, NY), F32),
            pltpu.VMEM((4, 8, NY), F32),
            pltpu.VMEM((2, CX, NY), F32),
            pltpu.VMEM((NG, 2, CX, NY), F32),
            pltpu.VMEM((2, CX, NY), F32),
            pltpu.VMEM((NG, 2, CX, NY), F32),
            pltpu.SMEM((1, 1, 6), jnp.int32),
            pltpu.SMEM((1, 1), jnp.int32),
            dma((5,)),
            dma((2,)), dma((2,)),
            dma((2,)), dma((2,)),
            dma((4,)), dma((4,)),
            dma((3,)), dma((NG,)),
            dma((3,)), dma((NG,)),
        ],
        compiler_params=pltpu.CompilerParams(
            collective_id=0, has_side_effects=True, vmem_limit_bytes=32 * 1024 * 1024
        ),
    )(phase, old, solute, blocks, count)


def solution(mesh):
    spec = P("growth", "lateral", None)
    return jax.shard_map(
        step,
        mesh=mesh,
        in_specs=(spec, spec, spec, spec, P("growth", "lateral")),
        out_specs=spec,
        check_vma=False,
    )
```

time: 82 us -> 19.6 us (0.24)
  starting transfers between devices: 24.1 us -> 0 us
  other arithmetic: 22.1 us -> 0 us
  Pallas kernels: 0 us -> 14.8 us
  blocking collectives: 14.1 us -> 0 us
  local copies, waits for them, and re-layouts: 13.4 us -> 3.92 us
  waiting for transfers between devices: 6.46 us -> 0 us
    ppermute x8 -> x0, starting transfers between devices: 24.1 us -> none  [the longest x4 12.3 us: with_halo(): lax.ppermute(head, axis, [((i + 1) % count, i) for i in range(ends)])]
    pallas_call x0 -> x1, Pallas kernels: none -> 14.8 us  [step(): pl.pallas_call(kernel, out_shape=jax.ShapeDtypeStruct((CZ, CX, NY), F32),...]
    all_gather x1 -> x0, blocking collectives: 14.1 us -> none  [shards(): gathered = lax.all_gather(boundary[None], 'growth', axis=0, tiled=True)]
    ppermute x8 -> x0, waiting for transfers between devices: 6.46 us -> none  [the longest x4 5.31 us: with_halo(): lax.ppermute(tail, axis, [(i, (i + 1) % count) for i in range(ends)])]
    sub x10 -> x0, other arithmetic: 4.37 us -> none  [the longest x4 2.62 us: local_solve(): right_sides - left_ratio[None] * lower_rows(right_sides, stride, 0.0)]
    gather x1 -> x0, local copies, waits for them, and re-layouts: 3.71 us -> none  [shards(): chosen = jnp.take(features, block_ids, axis=1)]
    mul x12 -> x0, other arithmetic: 3.44 us -> none  [the longest x1 1.31 us: shards(): flux_part * live_mask[None, :, None, None, None]]
    slice x20 -> x0, local copies, waits for them, and re-layouts: 3.23 us -> none  [the longest x10 2.15 us: lower_rows(): return jnp.concatenate([head_block, values[..., :-stride, :, :]], axis=-3)]
  transfers between devices with their start and end apart: 8 -> 0, of which waited for: 3 -> 0; matrix products, arithmetic and copies ran while one was open for 8% -> 0% of each run, Pallas kernels for 0% -> 0%
where the time goes in v1:
time: 19.6 us; the launch traced here: 19.4 us
  Pallas kernels  14.8 us (76%)
  local copies, waits for them, and re-layouts  3.92 us (20%)
  between operations  0.69 us (4%)
    pallas_call x1, Pallas kernels, step(): pl.pallas_call(kernel, out_shape=jax.ShapeDtypeStruct((CZ, CX, NY), F32),...  14.8 us
    unnamed x9, local copies, waits for them, and re-layouts  3.92 us

profile of v1, /device:TPU:96, one launch (start us, length us, event | category | flops | bytes accessed | tf_op | source)
XLA Modules:
  0.0 19.4 jit_solution(9194863678386987029)
XLA Ops:
  0.0 0.0 copy-start.3
  0.7 0.0 copy-done.3
  0.7 0.0 copy-start
  0.7 1.0 %copy-done = f32[32,32,128]{2,1,0:T(8,128)S(1)} copy-done((f32[32,32,128]{2,1,0:T(8,128)S(1)}, f32[32,32,128]{2,1,0:T(8,128)}, u32[]{:S(2)}) %copy-start) | copy-done | bytes 524312
  1.7 0.0 copy-start.1
  1.7 1.0 %copy-done.1 = f32[32,32,128]{2,1,0:T(8,128)S(1)} copy-done((f32[32,32,128]{2,1,0:T(8,128)S(1)}, f32[32,32,128]{2,1,0:T(8,128)}, u32[]{:S(2)}) %copy-start.1) | copy-done | bytes 524312
  2.8 0.0 copy-start.2
  2.8 1.0 %copy-done.2 = f32[32,32,128]{2,1,0:T(8,128)S(1)} copy-done((f32[32,32,128]{2,1,0:T(8,128)S(1)}, f32[32,32,128]{2,1,0:T(8,128)}, u32[]{:S(2)}) %copy-start.2) | copy-done | bytes 524312
  3.8 14.8 %shard_map.55 = f32[32,32,128]{2,1,0:T(8,128)S(1)} custom-call(f32[32,32,128]{2,1,0:T(8,128)S(1)} %copy-done, f32[32,32,128]{2,1,0:T(8,128)S(1)} %copy-done.1, f32[32,32,128]{2,1,0:T(8,128)S(1)} %copy-done.2, s32[1,1,6]{2,1,0:T(1,128)S(1)} %copy-done.3, s32[1,1]{1,0:T(1,128)S(6)} %copy.7.count), custom_call_target="tpu_custom_call" | custom-call | tf_op jit(solution)/shard_map/pallas_call | solution.py:358
  18.6 0.8 %copy.8 = f32[32,32,128]{2,1,0:T(8,128)} copy(f32[32,32,128]{2,1,0:T(8,128)S(1)} %shard_map.55) | data formatting | bytes 1048576
Async XLA Ops:
  0.0 0.7 %copy-start.3 = (s32[1,1,6]{2,1,0:T(1,128)S(1)}, s32[1,1,6]{2,1,0:T(1,128)}, u32[]{:S(2)}) copy-start(s32[1,1,6]{2,1,0:T(1,128)} %blocks.1) | copy-start | bytes 76
  0.7 1.0 %copy-start = (f32[32,32,128]{2,1,0:T(8,128)S(1)}, f32[32,32,128]{2,1,0:T(8,128)}, u32[]{:S(2)}) copy-start(f32[32,32,128]{2,1,0:T(8,128)} %phase.1) | copy-start | bytes 1572868
  1.7 1.0 %copy-start.1 = (f32[32,32,128]{2,1,0:T(8,128)S(1)}, f32[32,32,128]{2,1,0:T(8,128)}, u32[]{:S(2)}) copy-start(f32[32,32,128]{2,1,0:T(8,128)} %old.1) | copy-start | bytes 1572868
  2.8 1.0 %copy-start.2 = (f32[32,32,128]{2,1,0:T(8,128)S(1)}, f32[32,32,128]{2,1,0:T(8,128)}, u32[]{:S(2)}) copy-start(f32[32,32,128]{2,1,0:T(8,128)} %solute.1) | copy-start | bytes 1572868

commit v2 on v1

v2 whole, which is shorter than its diff:
```python
import jax
import jax.numpy as jnp
from jax import lax
from jax.experimental import pallas as pl
from jax.experimental.pallas import tpu as pltpu
from jax.sharding import PartitionSpec as P

BZ = 4
MESH = pl.DeviceIdType.MESH
NG = 4
NL = 32
CZ = 32
CX = 32
NY = 128
PAD = 8
ROW = CX + 2 * PAD
F32 = jnp.float32


def flux_factor(gx, gy, gz, pre):
    x2 = gx * gx
    y2 = gy * gy
    z2 = gz * gz
    inv = lax.rsqrt(x2 + y2 + z2 + 1.0)
    inv2 = inv * inv
    quartic = x2 * x2 + y2 * y2 + z2 * z2
    return pre * inv * (0.1 + 1.2 * quartic * (inv2 * inv2))


def next_y(a, last):
    return jnp.where(last, 0.0, pltpu.roll(a, NY - 1, 1))


def prev_y(a, first):
    return jnp.where(first, 0.0, pltpu.roll(a, 1, 1))


def kernel(
    phase, old, solute, blocks, count, out,
    ph, so, po, s0, fx, fz, rh, ee, bb, wf, pf, vb, qf, dd, pp, qq, ea, eb,
    cin, cnx, cout, cs0, cgy, cgz, cfa, cfz, cpq,
    xs, xr, zs, zr, cs, cr, gs, gr, pvs, pvr, es, er, blk, cnt,
    in_sem, x_ss, x_rs, z_ss, z_rs, c_ss, c_rs, g_ss, g_rs, pv_ss, pv_rs, e_ss, e_rs,
):
    g = lax.axis_index("growth")
    l = lax.axis_index("lateral")
    has_lo, has_hi = g > 0, g < NG - 1
    has_xl, has_xr = l > 0, l < NL - 1
    g_lo, g_hi = jnp.maximum(g - 1, 0), jnp.minimum(g + 1, NG - 1)
    l_lo, l_hi = jnp.maximum(l - 1, 0), jnp.minimum(l + 1, NL - 1)
    others = [lax.rem(g + d, NG) for d in range(1, NG)]

    barrier = pltpu.get_barrier_semaphore()

    def greet(cond, dev):
        @pl.when(cond)
        def _():
            pl.semaphore_signal(barrier, inc=1, device_id=dev, device_id_type=MESH)

    diag = [
        (has_lo & has_xl, (g_lo, l_lo)),
        (has_lo & has_xr, (g_lo, l_hi)),
        (has_hi & has_xl, (g_hi, l_lo)),
        (has_hi & has_xr, (g_hi, l_hi)),
    ]
    greet(has_xl, (g, l_lo))
    greet(has_xr, (g, l_hi))
    for cond, dev in diag:
        greet(cond, dev)
    for o in others:
        pl.semaphore_signal(barrier, inc=1, device_id=(o, l), device_id_type=MESH)

    ins = [
        pltpu.make_async_copy(phase, ph.at[pl.ds(1, CZ), pl.ds(PAD, CX), :], in_sem.at[0]),
        pltpu.make_async_copy(old, po, in_sem.at[1]),
        pltpu.make_async_copy(solute, so.at[:, pl.ds(PAD, CX), :], in_sem.at[2]),
        pltpu.make_async_copy(blocks, blk, in_sem.at[3]),
        pltpu.make_async_copy(count, cnt, in_sem.at[4]),
    ]
    for c in ins:
        c.start()

    lane = lax.broadcasted_iota(jnp.int32, (CX, NY), 1)
    row = lax.broadcasted_iota(jnp.int32, (CX, NY), 0)
    first, last = lane == 0, lane == NY - 1
    inner = (row > 0) & (row < CX - 1)
    zero = jnp.zeros((CX, NY), F32)
    one = zero + 1.0
    EXT = 40
    lane_e = lax.broadcasted_iota(jnp.int32, (EXT, NY), 1)
    first_e, last_e = lane_e == 0, lane_e == NY - 1

    def face(a, b):
        return 220.0 - 90.0 * (a + b)

    def coupling(a, b):
        return 0.055 - 0.0225 * (a + b)

    def ydiff(a):
        return next_y(a, last) - prev_y(a, first)

    def phz(z, off=0):
        return ph[z + 1, pl.ds(PAD + off, CX), :]

    def soz(z, off=0):
        return so[z, pl.ds(PAD + off, CX), :]

    for side, x in ((0, -1), (1, CX)):
        ph[0:CZ, PAD + x, :] = zero
        ph[CZ:CZ + 2, PAD + x, :] = zero[0:2]
        fx[:, PAD + x, :] = zero
        for buf in (cin, cnx, cout, cs0):
            buf[side, 0:8] = zero[0:8]
            buf[side, 40:56] = zero[0:16]
        @pl.when(jnp.logical_not((has_xl, has_xr)[side]))
        def _():
            xr[side] = jnp.zeros((4, CZ, NY), F32)
        @pl.when(jnp.logical_not((has_lo, has_hi)[side]))
        def _():
            zr[side] = jnp.zeros((3, CX, NY), F32)
    for i, (cond, _) in enumerate(diag):
        @pl.when(jnp.logical_not(cond))
        def _():
            cr[i] = jnp.zeros((8, NY), F32)

    for c in ins:
        c.wait()

    def prefactor(k, _):
        hit = jnp.int32(0)
        for s in range(6):
            hit = hit | jnp.where((blk[0, 0, s] == k) & (s < cnt[0, 0]), 1, 0)
        mask = hit.astype(F32) * 0.25
        for r in range(BZ):
            z = k * BZ + r
            s0[z] = (1.0 + 0.7 * soz(z)) * (phz(z) - po[z]) * mask
        return 0

    lax.fori_loop(0, CZ // BZ, prefactor, 0)

    for side, x in ((0, 0), (1, CX - 1)):
        near = 1 if x == 0 else CX - 2
        xs[side, 0] = ph[1:CZ + 1, PAD + x, :]
        xs[side, 1] = ph[1:CZ + 1, PAD + near, :]
        edge = so[:, PAD + x, :]
        xs[side, 2] = edge
        so[:, PAD + (-1 if side == 0 else CX), :] = edge
        xs[side, 3] = s0[:, x, :]
    for side, z in ((0, 0), (1, CZ - 1)):
        zs[side, 0] = phz(z)
        zs[side, 1] = phz(1 if z == 0 else CZ - 2)
        zs[side, 2] = s0[z]
        cs[2 * side] = phz(z)[0:8]
        cs[2 * side + 1] = phz(z)[CX - 8:CX]

    bottom = jnp.where(g == 0, face(phz(0), 0.0), zero) + 1.0
    top = jnp.where(g == NG - 1, face(phz(CZ - 1), 0.0), zero) + 1.0
    ea[0] = bottom
    pf[0] = one
    eb[CZ - 1] = top
    qf[CZ - 1] = one

    def eliminate(i, carry):
        e, prod, ebar, qprod = carry
        j = CZ - 1 - i
        u = face(phz(i), phz(i + 1))
        v = face(phz(j), phz(j - 1))
        w = u / (u + e)
        y = v / (v + ebar)
        e = 1.0 + w * e
        ebar = 1.0 + y * ebar
        prod = prod * w
        qprod = qprod * y
        wf[i] = w
        vb[j] = y
        ea[i + 1] = e
        eb[j - 1] = ebar
        pf[i + 1] = prod
        qf[j - 1] = qprod
        return e, prod, ebar, qprod

    def eliminate3(k, carry):
        for r in range(3):
            carry = eliminate(1 + 3 * k + r, carry)
        return carry

    lax.fori_loop(0, 10, eliminate3, eliminate(0, (bottom, one, top, one)))

    def finish(k, _):
        for r in range(BZ):
            i = k * BZ + r
            d = 1.0 / (ea[i] + eb[i] - 1.0)
            dd[i] = d
            pp[i] = pf[i] * d
            qq[i] = qf[i] * d
        return 0

    lax.fori_loop(0, CZ // BZ, finish, 0)
    gs[0] = pp[0]
    gs[1] = qq[CZ - 1]
    gs[2] = pp[CZ - 1]
    gs[3] = phz(0)
    gs[4] = phz(CZ - 1)
    gr[g] = gs[...]

    both = has_lo.astype(jnp.int32) + has_hi.astype(jnp.int32) + 1
    pl.semaphore_wait(
        barrier, NG - 1 + (has_xl.astype(jnp.int32) + has_xr.astype(jnp.int32)) * both
    )

    def remote(src, dst, ss, rs, dev):
        return pltpu.make_async_remote_copy(
            src_ref=src, dst_ref=dst, send_sem=ss, recv_sem=rs, device_id=dev, device_id_type=MESH
        )

    x_out = [
        (has_xl, remote(xs.at[0], xr.at[1], x_ss.at[0], x_rs.at[1], (g, l_lo))),
        (has_xr, remote(xs.at[1], xr.at[0], x_ss.at[1], x_rs.at[0], (g, l_hi))),
    ]
    z_out = [
        (has_lo, remote(zs.at[0], zr.at[1], z_ss.at[0], z_rs.at[1], (g_lo, l))),
        (has_hi, remote(zs.at[1], zr.at[0], z_ss.at[1], z_rs.at[0], (g_hi, l))),
    ]
    c_out = [
        (cond, remote(cs.at[i], cr.at[3 - i], c_ss.at[i], c_rs.at[3 - i], dev))
        for i, (cond, dev) in enumerate(diag)
    ]
    for cond, cp in x_out + z_out + c_out:
        pl.when(cond)(cp.start)
    x_in = [
        (has_xl, remote(xs.at[1], xr.at[0], x_ss.at[1], x_rs.at[0], (g, l_lo))),
        (has_xr, remote(xs.at[0], xr.at[1], x_ss.at[0], x_rs.at[1], (g, l_hi))),
    ]
    z_in = [
        (has_lo, remote(zs.at[1], zr.at[0], z_ss.at[1], z_rs.at[0], (g_lo, l))),
        (has_hi, remote(zs.at[0], zr.at[1], z_ss.at[0], z_rs.at[1], (g_hi, l))),
    ]
    c_in = [
        (cond, remote(cs.at[3 - i], cr.at[i], c_ss.at[3 - i], c_rs.at[i], dev))
        for i, (cond, dev) in enumerate(diag)
    ]

    def spread(src, dst, ss, rs):
        cps = [remote(src, dst.at[g], ss.at[d], rs.at[g], (o, l)) for d, o in enumerate(others)]
        for cp in cps:
            cp.start()
        return cps

    def arrive(src, dst, ss, rs):
        for o in others:
            remote(src, dst.at[o], ss.at[0], rs.at[o], (o, l)).wait_recv()

    def plane(z):
        here = phz(z)
        right, left = phz(z, 1), phz(z, -1)
        yn, yp = next_y(here, last), prev_y(here, first)
        gx = right - left
        gy = yn - yp
        gz = phz(z + 1) - phz(z - 1)
        factor = flux_factor(gx, gy, gz, jnp.where(inner, s0[z], 0.0))
        fx[z, pl.ds(PAD, CX), :] = factor * gx
        fz[z + 1] = factor * gz
        flux_y = factor * gy
        s = soz(z)
        side = coupling(here, right) * (soz(z, 1) - s) + coupling(here, left) * (soz(z, -1) - s)
        side = side + coupling(here, yn) * (next_y(s, last) - s)
        side = side + coupling(here, yp) * (prev_y(s, first) - s)
        rh[z] = s + side + ydiff(flux_y)

    def gather_rhs(z, sums):
        r = (
            rh[z]
            + (fx[z, pl.ds(PAD + 1, CX), :] - fx[z, pl.ds(PAD - 1, CX), :])
            + (fz[z + 2] - fz[z])
        )
        rh[z] = r
        return sums[0] + pp[z] * r, sums[1] + qq[z] * r

    def planes(k, _):
        for r in range(3):
            plane(1 + 3 * k + r)
        return 0

    lax.fori_loop(0, 10, planes, 0)

    g_out = spread(gs, gr, g_ss, g_rs)

    def rows(k, sums):
        for r in range(BZ):
            sums = gather_rhs(2 + BZ * k + r, sums)
        return sums

    sums = lax.fori_loop(0, 7, rows, (zero, zero))

    for side, x in ((0, 0), (1, CX - 1)):
        near = 1 if x == 0 else CX - 2
        cin[side, 8:40] = xs[side, 0]
        cnx[side, 8:40] = xs[side, 1]
        cs0[side, 8:40] = xs[side, 3]
        cpq[side, 0] = pp[:, x, :]
        cpq[side, 1] = qq[:, x, :]
        cpq[side, 2] = pp[:, near, :]
        cpq[side, 3] = qq[:, near, :]

    for cond, cp in z_in:
        pl.when(cond)(cp.wait_recv)
    ph[0, pl.ds(PAD, CX), :] = zr[0, 0]
    ph[CZ + 1, pl.ds(PAD, CX), :] = zr[1, 0]
    for side, z in ((0, -1), (1, CZ)):
        gz = phz(0) - zr[side, 1] if side == 0 else zr[side, 1] - phz(CZ - 1)
        gx = phz(z, 1) - phz(z, -1)
        factor = flux_factor(gx, ydiff(zr[side, 0]), gz, jnp.where(inner, zr[side, 2], 0.0))
        fz[z + 1] = factor * gz
    plane(0)
    plane(CZ - 1)
    for z in (0, 1, CZ - 2, CZ - 1):
        sums = gather_rhs(z, sums)
    pvs[0] = sums[0]
    pvs[1] = sums[1]
    pvr[g] = pvs[...]
    pv_out = spread(pvs, pvr, pv_ss, pv_rs)

    for side, x in ((0, 0), (1, CX - 1)):
        near = 1 if x == 0 else CX - 2
        for buf, which, xx in ((cin, 0, x), (cnx, 0, near), (cs0, 2, x)):
            buf[side, 7:8] = zr[0, which, xx:xx + 1, :]
            buf[side, 40:41] = zr[1, which, xx:xx + 1, :]
        cin[side, 6:7] = zr[0, 1, x:x + 1, :]
        cin[side, 41:42] = zr[1, 1, x:x + 1, :]
        a = cin[side, 7:47]
        cgy[side] = next_y(a, last_e) - prev_y(a, first_e)
        cgz[side] = cin[side, 8:48] - cin[side, 6:46]

    for cond, cp in x_in + c_in:
        pl.when(cond)(cp.wait_recv)
    sub = lax.broadcasted_iota(jnp.int32, (8, NY), 0)
    tile_p = jnp.zeros((8, NY), F32)
    tile_q = jnp.zeros((8, NY), F32)
    for side, x in ((0, 0), (1, CX - 1)):
        near = 1 if x == 0 else CX - 2
        pick = slice(7, 8) if side == 0 else slice(0, 1)
        outer = xr[side, 0]
        cout[side, 7:8] = cr[side, pick]
        cout[side, 8:40] = outer
        cout[side, 40:41] = cr[2 + side, pick]
        gin = cnx[side, 7:47] - cout[side, 7:47]
        factor = flux_factor(gin, cgy[side], cgz[side], cs0[side, 7:47])
        cfa[side] = factor
        cfz[side] = factor * cgz[side]
        g_out2 = xs[side, 0] - xr[side, 1]
        f_out = flux_factor(
            g_out2, ydiff(outer), cout[side, 9:41] - cout[side, 7:39], xr[side, 3]
        ) * g_out2
        own = cfa[side, 1:33]
        d_near = -own * (xs[side, 1] - outer)
        d_edge = (
            coupling(xs[side, 0], outer) * (xr[side, 2] - xs[side, 2])
            - f_out
            + ydiff(own * cgy[side, 1:33])
            + (cfz[side, 2:34] - cfz[side, 0:32])
        )
        at, at_near = (0, 1) if side == 0 else (7, 6)
        for d, where, k in ((d_edge, at, 0), (d_near, at_near, 2)):
            tile_p = jnp.where(sub == where, jnp.sum(cpq[side, k] * d, axis=0, keepdims=True), tile_p)
            tile_q = jnp.where(sub == where, jnp.sum(cpq[side, k + 1] * d, axis=0, keepdims=True), tile_q)
        cfa[side, 0:32] = d_edge
        cfz[side, 0:32] = d_near
    es[0] = tile_p
    es[1] = tile_q
    er[g] = es[...]
    e_out = spread(es, er, e_ss, e_rs)
    for side, x in ((0, 0), (1, CX - 1)):
        near = 1 if x == 0 else CX - 2
        rh[:, x, :] = rh[:, x, :] + cfa[side, 0:32]
        rh[:, near, :] = rh[:, near, :] + cfz[side, 0:32]

    ee[0] = rh[0]
    bb[CZ - 1] = rh[CZ - 1]

    def sweep(i, carry):
        f, b = carry
        j = CZ - 1 - i
        f = rh[i] + wf[i - 1] * f
        b = rh[j] + vb[j + 1] * b
        ee[i] = f
        bb[j] = b
        return f, b

    def sweep3(k, carry):
        for r in range(3):
            carry = sweep(2 + 3 * k + r, carry)
        return carry

    lax.fori_loop(0, 10, sweep3, sweep(1, (rh[0], rh[CZ - 1])))

    def local(k, _):
        for r in range(BZ):
            z = k * BZ + r
            ee[z] = (ee[z] + bb[z] - rh[z]) * dd[z]
        return 0

    lax.fori_loop(0, CZ // BZ, local, 0)

    arrive(gs, gr, g_ss, g_rs)

    def self_term(k):
        return 1.0 / face(gr[k, 4], gr[k + 1, 3]) + gr[k, 1] + gr[k + 1, 0]

    m0 = 1.0 / self_term(0)
    t1, t2 = gr[1, 2], gr[2, 2]
    k1 = t1 * m0
    m1 = 1.0 / (self_term(1) - t1 * k1)
    k2 = t2 * m1
    m2 = 1.0 / (self_term(2) - t2 * k2)
    arrive(pvs, pvr, pv_ss, pv_rs)
    jump = [pvr[k, 1] - pvr[k + 1, 0] for k in range(NG - 1)]
    arrive(es, er, e_ss, e_rs)
    for k in range(NG - 1):
        tile = er[k, 1] - er[k + 1, 0]
        full = jnp.concatenate([tile, jnp.zeros((CX - 16, NY), F32), tile], axis=0)
        jump[k] = jump[k] + jnp.where((row < 2) | (row >= CX - 2), full, 0.0)
    b0 = jump[0]
    b1 = jump[1] + k1 * b0
    b2 = jump[2] + k2 * b1
    q2 = b2 * m2
    q1 = b1 * m1 + k2 * q2
    q0 = b0 * m0 + k1 * q1
    below = jnp.where(g == 1, q0, jnp.where(g == 2, q1, jnp.where(g == 3, q2, 0.0)))
    above = jnp.where(g == 0, q0, jnp.where(g == 1, q1, jnp.where(g == 2, q2, 0.0)))

    def close(k, _):
        for r in range(BZ):
            z = k * BZ + r
            out[z] = ee[z] + pp[z] * below - qq[z] * above
        return 0

    lax.fori_loop(0, CZ // BZ, close, 0)

    for cond, cp in x_out + z_out + c_out:
        pl.when(cond)(cp.wait_send)
    for cp in g_out + pv_out + e_out:
        cp.wait_send()


def step(phase, old, solute, blocks, count):
    def buf(*shape):
        return pltpu.VMEM(shape + (NY,), F32)

    slab = buf(CZ, CX)
    dma = pltpu.SemaphoreType.DMA
    return pl.pallas_call(
        kernel,
        out_shape=pltpu.VMEM((CZ, CX, NY), F32),
        in_specs=[pl.BlockSpec(memory_space=pl.ANY)] * 5,
        out_specs=pl.BlockSpec(memory_space=pltpu.VMEM),
        scratch_shapes=[
            buf(CZ + 2, ROW), buf(CZ, ROW), slab, slab, buf(CZ, ROW), buf(CZ + 2, CX),
            slab, slab, slab, slab, slab, slab, slab, slab, slab, slab, slab, slab,
            buf(2, 56), buf(2, 56), buf(2, 56), buf(2, 56),
            buf(2, 40), buf(2, 40), buf(2, 40), buf(2, 40), buf(2, 4, CZ),
            buf(2, 4, CZ), buf(2, 4, CZ),
            buf(2, 3, CX), buf(2, 3, CX),
            buf(4, 8), buf(4, 8),
            buf(5, CX), buf(NG, 5, CX),
            buf(2, CX), buf(NG, 2, CX),
            buf(2, 8), buf(NG, 2, 8),
            pltpu.SMEM((1, 1, 6), jnp.int32),
            pltpu.SMEM((1, 1), jnp.int32),
            dma((5,)),
            dma((2,)), dma((2,)),
            dma((2,)), dma((2,)),
            dma((4,)), dma((4,)),
            dma((3,)), dma((NG,)),
            dma((3,)), dma((NG,)),
            dma((3,)), dma((NG,)),
        ],
        compiler_params=pltpu.CompilerParams(
            collective_id=0, has_side_effects=True, vmem_limit_bytes=66000000
        ),
    )(phase, old, solute, blocks, count)


def solution(mesh):
    spec = P("growth", "lateral", None)
    return jax.shard_map(
        step,
        mesh=mesh,
        in_specs=(spec, spec, spec, spec, P("growth", "lateral")),
        out_specs=spec,
        check_vma=False,
    )
```

time: 19.6 us -> 15.8 us (0.81)
  local copies, waits for them, and re-layouts: 3.92 us -> 0.8 us
  Pallas kernels: 14.8 us -> 14.1 us
    unnamed x9 -> x1, local copies, waits for them, and re-layouts: 3.92 us -> 0.8 us
    pallas_call x1, Pallas kernels: 14.8 us -> 14.1 us  [step(): pl.pallas_call(kernel, out_shape=pltpu.VMEM((CZ, CX, NY), F32), in_specs=...]
where the time goes in v2:
time: 15.8 us; the launch traced here: 15.6 us
  Pallas kernels  14.1 us (89%)
  local copies, waits for them, and re-layouts  0.8 us (5%)
  between operations  0.66 us (4%)
    pallas_call x1, Pallas kernels, step(): pl.pallas_call(kernel, out_shape=pltpu.VMEM((CZ, CX, NY), F32), in_specs=...  14.1 us
    unnamed x1, local copies, waits for them, and re-layouts  0.8 us

profile of v2, /device:TPU:96, one launch (start us, length us, event | category | flops | bytes accessed | tf_op | source)
XLA Modules:
  0.0 15.6 jit_solution(13767392030648651424)
XLA Ops:
  0.7 14.1 %shard_map.55 = f32[32,32,128]{2,1,0:T(8,128)S(1)} custom-call(f32[32,32,128]{2,1,0:T(8,128)} %phase.1, f32[32,32,128]{2,1,0:T(8,128)} %old.1, f32[32,32,128]{2,1,0:T(8,128)} %solute.1, s32[1,1,6]{2,1,0:T(1,128)} %blocks.1, s32[1,1]{1,0:T(1,128)S(6)} %copy.8.count), custom_call_target="tpu_custom_call" | custom-call | tf_op jit(solution)/shard_map/pallas_call | solution.py:451
  14.8 0.8 %copy.7 = f32[32,32,128]{2,1,0:T(8,128)} copy(f32[32,32,128]{2,1,0:T(8,128)S(1)} %shard_map.55) | data formatting | bytes 1048576

commit v3 on v2

--- a/solution.py
+++ b/solution.py
@@ -39,8 +39,8 @@
     phase, old, solute, blocks, count, out,
     ph, so, po, s0, fx, fz, rh, ee, bb, wf, pf, vb, qf, dd, pp, qq, ea, eb,
     cin, cnx, cout, cs0, cgy, cgz, cfa, cfz, cpq,
-    xs, xr, zs, zr, cs, cr, gs, gr, pvs, pvr, es, er, blk, cnt,
-    in_sem, x_ss, x_rs, z_ss, z_rs, c_ss, c_rs, g_ss, g_rs, pv_ss, pv_rs, e_ss, e_rs,
+    xs, xr, zs, zr, cs, cr, ts, tr, pvs, pvr, es, er, blk, cnt,
+    in_sem, x_ss, x_rs, z_ss, z_rs, c_ss, c_rs, t_ss, t_rs, pv_ss, pv_rs, e_ss, e_rs, met,
 ):
     g = lax.axis_index("growth")
     l = lax.axis_index("lateral")
@@ -48,7 +48,7 @@
     has_xl, has_xr = l > 0, l < NL - 1
     g_lo, g_hi = jnp.maximum(g - 1, 0), jnp.minimum(g + 1, NG - 1)
     l_lo, l_hi = jnp.maximum(l - 1, 0), jnp.minimum(l + 1, NL - 1)
-    others = [lax.rem(g + d, NG) for d in range(1, NG)]
+    others = [lax.rem(g + d, NG) for d in (2, 1, 3)]
 
     barrier = pltpu.get_barrier_semaphore()
 
@@ -63,12 +63,12 @@
         (has_hi & has_xl, (g_hi, l_lo)),
         (has_hi & has_xr, (g_hi, l_hi)),
     ]
+    ends = jnp.logical_not(has_lo & has_hi)
+    greet(has_lo, (g_lo, l))
+    greet(has_hi, (g_hi, l))
     greet(has_xl, (g, l_lo))
     greet(has_xr, (g, l_hi))
-    for cond, dev in diag:
-        greet(cond, dev)
-    for o in others:
-        pl.semaphore_signal(barrier, inc=1, device_id=(o, l), device_id_type=MESH)
+    greet(ends, (NG - 1 - g, l))
 
     ins = [
         pltpu.make_async_copy(phase, ph.at[pl.ds(1, CZ), pl.ds(PAD, CX), :], in_sem.at[0]),
@@ -105,53 +105,107 @@
     def soz(z, off=0):
         return so[z, pl.ds(PAD + off, CX), :]
 
-    for side, x in ((0, -1), (1, CX)):
-        ph[0:CZ, PAD + x, :] = zero
-        ph[CZ:CZ + 2, PAD + x, :] = zero[0:2]
-        fx[:, PAD + x, :] = zero
-        for buf in (cin, cnx, cout, cs0):
-            buf[side, 0:8] = zero[0:8]
-            buf[side, 40:56] = zero[0:16]
-        @pl.when(jnp.logical_not((has_xl, has_xr)[side]))
-        def _():
-            xr[side] = jnp.zeros((4, CZ, NY), F32)
-        @pl.when(jnp.logical_not((has_lo, has_hi)[side]))
-        def _():
-            zr[side] = jnp.zeros((3, CX, NY), F32)
-    for i, (cond, _) in enumerate(diag):
-        @pl.when(jnp.logical_not(cond))
-        def _():
-            cr[i] = jnp.zeros((8, NY), F32)
-
     for c in ins:
         c.wait()
 
-    def prefactor(k, _):
-        hit = jnp.int32(0)
-        for s in range(6):
-            hit = hit | jnp.where((blk[0, 0, s] == k) & (s < cnt[0, 0]), 1, 0)
-        mask = hit.astype(F32) * 0.25
-        for r in range(BZ):
-            z = k * BZ + r
-            s0[z] = (1.0 + 0.7 * soz(z)) * (phz(z) - po[z]) * mask
-        return 0
-
-    lax.fori_loop(0, CZ // BZ, prefactor, 0)
-
+    live = [jnp.where(s < cnt[0, 0], blk[0, 0, s], -1) for s in range(6)]
+
+    def masked(k):
+        hit = k == live[0]
+        for b in live[1:]:
+            hit = hit | (k == b)
+        return jnp.where(hit, 0.25, 0.0)
+
+    column_mask = masked(row // BZ)
     for side, x in ((0, 0), (1, CX - 1)):
         near = 1 if x == 0 else CX - 2
-        xs[side, 0] = ph[1:CZ + 1, PAD + x, :]
+        here, s = ph[1:CZ + 1, PAD + x, :], so[:, PAD + x, :]
+        xs[side, 0] = here
         xs[side, 1] = ph[1:CZ + 1, PAD + near, :]
-        edge = so[:, PAD + x, :]
-        xs[side, 2] = edge
-        so[:, PAD + (-1 if side == 0 else CX), :] = edge
-        xs[side, 3] = s0[:, x, :]
+        xs[side, 2] = s
+        xs[side, 3] = (1.0 + 0.7 * s) * (here - po[:, x, :]) * column_mask
     for side, z in ((0, 0), (1, CZ - 1)):
         zs[side, 0] = phz(z)
         zs[side, 1] = phz(1 if z == 0 else CZ - 2)
-        zs[side, 2] = s0[z]
+        zs[side, 2] = (1.0 + 0.7 * soz(z)) * (phz(z) - po[z]) * masked(jnp.int32(z // BZ))
         cs[2 * side] = phz(z)[0:8]
         cs[2 * side + 1] = phz(z)[CX - 8:CX]
+
+    def many(*conds):
+        return sum(c.astype(jnp.int32) for c in conds)
+
+    pl.semaphore_wait(barrier, many(has_lo, has_hi, has_xl, has_xr, ends))
+
+    def remote(src, dst, ss, rs, dev):
+        return pltpu.make_async_remote_copy(
+            src_ref=src, dst_ref=dst, send_sem=ss, recv_sem=rs, device_id=dev, device_id_type=MESH
+        )
+
+    x_out = [
+        (has_xl, remote(xs.at[0], xr.at[1], x_ss.at[0], x_rs.at[1], (g, l_lo))),
+        (has_xr, remote(xs.at[1], xr.at[0], x_ss.at[1], x_rs.at[0], (g, l_hi))),
+    ]
+    z_out = [
+        (has_lo, remote(zs.at[0, 0:3], zr.at[1, 0:3], z_ss.at[0], z_rs.at[1], (g_lo, l))),
+        (has_hi, remote(zs.at[1, 0:3], zr.at[0, 0:3], z_ss.at[1], z_rs.at[0], (g_hi, l))),
+    ]
+    w_out = [
+        (has_lo, remote(zs.at[0, 3], zr.at[1, 3], z_ss.at[2], z_rs.at[3], (g_lo, l))),
+        (has_hi, remote(zs.at[1, 3], zr.at[0, 3], z_ss.at[3], z_rs.at[2], (g_hi, l))),
+    ]
+    w_in = [
+        (has_lo, remote(zs.at[1, 3], zr.at[0, 3], z_ss.at[3], z_rs.at[2], (g_lo, l))),
+        (has_hi, remote(zs.at[0, 3], zr.at[1, 3], z_ss.at[2], z_rs.at[3], (g_hi, l))),
+    ]
+    c_out = [
+        (cond, remote(cs.at[i], cr.at[3 - i], c_ss.at[i], c_rs.at[3 - i], dev))
+        for i, (cond, dev) in enumerate(diag)
+    ]
+    for cond, cp in z_out + x_out:
+        pl.when(cond)(cp.start)
+    for i, (cond, o) in enumerate(((has_lo, g_lo), (has_hi, g_hi))):
+        @pl.when(cond)
+        def _():
+            pl.semaphore_signal(met, inc=1, device_id=(o, l), device_id_type=MESH)
+    x_in = [
+        (has_xl, remote(xs.at[1], xr.at[0], x_ss.at[1], x_rs.at[0], (g, l_lo))),
+        (has_xr, remote(xs.at[0], xr.at[1], x_ss.at[0], x_rs.at[1], (g, l_hi))),
+    ]
+    z_in = [
+        (has_lo, remote(zs.at[1, 0:3], zr.at[0, 0:3], z_ss.at[1], z_rs.at[0], (g_lo, l))),
+        (has_hi, remote(zs.at[0, 0:3], zr.at[1, 0:3], z_ss.at[0], z_rs.at[1], (g_hi, l))),
+    ]
+    c_in = [
+        (cond, remote(cs.at[3 - i], cr.at[i], c_ss.at[3 - i], c_rs.at[i], dev))
+        for i, (cond, dev) in enumerate(diag)
+    ]
+
+    middle = has_lo & has_hi
+    up = g >= NG // 2
+    half = up.astype(jnp.int32)
+    inner_dev, outer_dev = 1 + half, 3 * half
+    far_inner, far_outer = 2 - half, 3 - 3 * half
+    t_out, pv_out = [], []
+    for d, o in enumerate(others):
+        to_end = middle & (o == outer_dev)
+        to_far = middle & (o != outer_dev)
+        for cond, at in ((to_end, pl.ds(0, 2)), (to_far, pl.ds(1, 2))):
+            t_out.append((cond, remote(ts.at[at], tr.at[g, at], t_ss.at[d], t_rs.at[g], (o, l))))
+        for cond, at in ((to_end, pl.ds(0, 2)), (jnp.logical_not(to_end), pl.ds(2, 1))):
+            pv_out.append((cond, remote(pvs.at[at], pvr.at[g, at], pv_ss.at[d], pv_rs.at[g], (o, l))))
+    t_in, pv_in = [], []
+    for k in range(NG):
+        from_inner = jnp.logical_not(middle) & (inner_dev == k)
+        if k in (1, 2):
+            from_far = far_inner == k
+            for cond, at in ((from_inner, pl.ds(0, 2)), (from_far, pl.ds(1, 2))):
+                t_in.append((cond, remote(ts.at[at], tr.at[k, at], t_ss.at[0], t_rs.at[k], (k, l))))
+        from_other = (g != k) & jnp.logical_not(from_inner)
+        for cond, at in ((from_inner, pl.ds(0, 2)), (from_other, pl.ds(2, 1))):
+            pv_in.append((cond, remote(pvs.at[at], pvr.at[k, at], pv_ss.at[0], pv_rs.at[k], (k, l))))
+    e_out = [
+        (None, remote(es, er.at[g], e_ss.at[d], e_rs.at[g], (o, l))) for d, o in enumerate(others)
+    ]
 
     bottom = jnp.where(g == 0, face(phz(0), 0.0), zero) + 1.0
     top = jnp.where(g == NG - 1, face(phz(CZ - 1), 0.0), zero) + 1.0
@@ -196,59 +250,41 @@
         return 0
 
     lax.fori_loop(0, CZ // BZ, finish, 0)
-    gs[0] = pp[0]
-    gs[1] = qq[CZ - 1]
-    gs[2] = pp[CZ - 1]
-    gs[3] = phz(0)
-    gs[4] = phz(CZ - 1)
-    gr[g] = gs[...]
-
-    both = has_lo.astype(jnp.int32) + has_hi.astype(jnp.int32) + 1
-    pl.semaphore_wait(
-        barrier, NG - 1 + (has_xl.astype(jnp.int32) + has_xr.astype(jnp.int32)) * both
-    )
-
-    def remote(src, dst, ss, rs, dev):
-        return pltpu.make_async_remote_copy(
-            src_ref=src, dst_ref=dst, send_sem=ss, recv_sem=rs, device_id=dev, device_id_type=MESH
-        )
-
-    x_out = [
-        (has_xl, remote(xs.at[0], xr.at[1], x_ss.at[0], x_rs.at[1], (g, l_lo))),
-        (has_xr, remote(xs.at[1], xr.at[0], x_ss.at[1], x_rs.at[0], (g, l_hi))),
-    ]
-    z_out = [
-        (has_lo, remote(zs.at[0], zr.at[1], z_ss.at[0], z_rs.at[1], (g_lo, l))),
-        (has_hi, remote(zs.at[1], zr.at[0], z_ss.at[1], z_rs.at[0], (g_hi, l))),
-    ]
-    c_out = [
-        (cond, remote(cs.at[i], cr.at[3 - i], c_ss.at[i], c_rs.at[3 - i], dev))
-        for i, (cond, dev) in enumerate(diag)
-    ]
-    for cond, cp in x_out + z_out + c_out:
+    zs[0, 3] = pp[0]
+    zs[1, 3] = qq[CZ - 1]
+    ts[1] = pp[CZ - 1]
+    pl.semaphore_wait(met, many(has_lo, has_hi))
+    for cond, cp in c_out + w_out:
         pl.when(cond)(cp.start)
-    x_in = [
-        (has_xl, remote(xs.at[1], xr.at[0], x_ss.at[1], x_rs.at[0], (g, l_lo))),
-        (has_xr, remote(xs.at[0], xr.at[1], x_ss.at[0], x_rs.at[1], (g, l_hi))),
-    ]
-    z_in = [
-        (has_lo, remote(zs.at[1], zr.at[0], z_ss.at[1], z_rs.at[0], (g_lo, l))),
-        (has_hi, remote(zs.at[0], zr.at[1], z_ss.at[0], z_rs.at[1], (g_hi, l))),
-    ]
-    c_in = [
-        (cond, remote(cs.at[3 - i], cr.at[i], c_ss.at[3 - i], c_rs.at[i], dev))
-        for i, (cond, dev) in enumerate(diag)
-    ]
-
-    def spread(src, dst, ss, rs):
-        cps = [remote(src, dst.at[g], ss.at[d], rs.at[g], (o, l)) for d, o in enumerate(others)]
-        for cp in cps:
-            cp.start()
-        return cps
-
-    def arrive(src, dst, ss, rs):
-        for o in others:
-            remote(src, dst.at[o], ss.at[0], rs.at[o], (o, l)).wait_recv()
+
+
+    for side, x in ((0, -1), (1, CX)):
+        ph[0:CZ, PAD + x, :] = zero
+        ph[CZ:CZ + 2, PAD + x, :] = zero[0:2]
+        fx[:, PAD + x, :] = zero
+        so[:, PAD + x, :] = xs[side, 2]
+        for buf in (cin, cnx, cout, cs0):
+            buf[side, 0:8] = zero[0:8]
+            buf[side, 40:56] = zero[0:16]
+        @pl.when(jnp.logical_not((has_xl, has_xr)[side]))
+        def _():
+            xr[side] = jnp.zeros((4, CZ, NY), F32)
+        @pl.when(jnp.logical_not((has_lo, has_hi)[side]))
+        def _():
+            zr[side] = jnp.zeros((4, CX, NY), F32)
+    for i, (cond, _) in enumerate(diag):
+        @pl.when(jnp.logical_not(cond))
+        def _():
+            cr[i] = jnp.zeros((8, NY), F32)
+
+    def prefactor(k, _):
+        mask = masked(k)
+        for r in range(BZ):
+            z = k * BZ + r
+            s0[z] = (1.0 + 0.7 * soz(z)) * (phz(z) - po[z]) * mask
+        return 0
+
+    lax.fori_loop(0, CZ // BZ, prefactor, 0)
 
     def plane(z):
         here = phz(z)
@@ -263,9 +299,9 @@
         flux_y = factor * gy
         s = soz(z)
         side = coupling(here, right) * (soz(z, 1) - s) + coupling(here, left) * (soz(z, -1) - s)
-        side = side + coupling(here, yn) * (next_y(s, last) - s)
-        side = side + coupling(here, yp) * (prev_y(s, first) - s)
-        rh[z] = s + side + ydiff(flux_y)
+        step_y = coupling(here, yn) * (next_y(s, last) - s)
+        back = jnp.where(first, coupling(here, 0.0) * s, pltpu.roll(step_y + flux_y, 1, 1))
+        rh[z] = s + side + (step_y + next_y(flux_y, last) - back)
 
     def gather_rhs(z, sums):
         r = (
@@ -277,13 +313,11 @@
         return sums[0] + pp[z] * r, sums[1] + qq[z] * r
 
     def planes(k, _):
-        for r in range(3):
-            plane(1 + 3 * k + r)
+        for r in range(6):
+            plane(1 + 6 * k + r)
         return 0
 
-    lax.fori_loop(0, 10, planes, 0)
-
-    g_out = spread(gs, gr, g_ss, g_rs)
+    lax.fori_loop(0, 5, planes, 0)
 
     def rows(k, sums):
         for r in range(BZ):
@@ -304,6 +338,18 @@
 
     for cond, cp in z_in:
         pl.when(cond)(cp.wait_recv)
+    for cond, cp in w_in:
+        pl.when(cond)(cp.wait_recv)
+    self_hi = 1.0 / face(phz(CZ - 1), zr[1, 0]) + qq[CZ - 1] + zr[1, 3]
+    self_lo = 1.0 / face(phz(0), zr[0, 0]) + pp[0] + zr[0, 3]
+    even = lax.rem(g, 2) == 0
+    self_out = jnp.where(even, self_hi, self_lo)
+    ts[0] = jnp.where(even, self_lo, self_hi)
+    ts[2] = self_out
+    tr[g] = ts[...]
+    for cond, cp in t_out:
+        pl.when(cond)(cp.start)
+    own_k = ts[1] / self_out
     ph[0, pl.ds(PAD, CX), :] = zr[0, 0]
     ph[CZ + 1, pl.ds(PAD, CX), :] = zr[1, 0]
     for side, z in ((0, -1), (1, CZ)):
@@ -315,10 +361,13 @@
     plane(CZ - 1)
     for z in (0, 1, CZ - 2, CZ - 1):
         sums = gather_rhs(z, sums)
-    pvs[0] = sums[0]
-    pvs[1] = sums[1]
+    facing, away = jnp.where(up, sums[0], sums[1]), jnp.where(up, sums[1], sums[0])
+    pvs[0] = facing
+    pvs[1] = away
+    pvs[2] = jnp.where(middle, facing - own_k * away, facing)
     pvr[g] = pvs[...]
-    pv_out = spread(pvs, pvr, pv_ss, pv_rs)
+    for cond, cp in pv_out:
+        pl.when(cond)(cp.start)
 
     for side, x in ((0, 0), (1, CX - 1)):
         near = 1 if x == 0 else CX - 2
@@ -365,10 +414,15 @@
             tile_q = jnp.where(sub == where, jnp.sum(cpq[side, k + 1] * d, axis=0, keepdims=True), tile_q)
         cfa[side, 0:32] = d_edge
         cfz[side, 0:32] = d_near
-    es[0] = tile_p
-    es[1] = tile_q
+    left_rows = sub < 4
+    tile_facing, tile_away = jnp.where(up, tile_p, tile_q), jnp.where(up, tile_q, tile_p)
+    tile_k = jnp.where(left_rows, own_k[0:8], own_k[CX - 8:CX])
+    es[0] = tile_facing
+    es[1] = tile_away
+    es[2] = jnp.where(middle, tile_facing - tile_k * tile_away, tile_facing)
     er[g] = es[...]
-    e_out = spread(es, er, e_ss, e_rs)
+    for _, cp in e_out:
+        cp.start()
     for side, x in ((0, 0), (1, CX - 1)):
         near = 1 if x == 0 else CX - 2
         rh[:, x, :] = rh[:, x, :] + cfa[side, 0:32]
@@ -401,32 +455,31 @@
 
     lax.fori_loop(0, CZ // BZ, local, 0)
 
-    arrive(gs, gr, g_ss, g_rs)
-
-    def self_term(k):
-        return 1.0 / face(gr[k, 4], gr[k + 1, 3]) + gr[k, 1] + gr[k + 1, 0]
-
-    m0 = 1.0 / self_term(0)
-    t1, t2 = gr[1, 2], gr[2, 2]
-    k1 = t1 * m0
-    m1 = 1.0 / (self_term(1) - t1 * k1)
-    k2 = t2 * m1
-    m2 = 1.0 / (self_term(2) - t2 * k2)
-    arrive(pvs, pvr, pv_ss, pv_rs)
-    jump = [pvr[k, 1] - pvr[k + 1, 0] for k in range(NG - 1)]
-    arrive(es, er, e_ss, e_rs)
-    for k in range(NG - 1):
-        tile = er[k, 1] - er[k + 1, 0]
+    for cond, cp in t_in:
+        pl.when(cond)(cp.wait_recv)
+    t_far, t_own = tr[far_inner, 1], tr[inner_dev, 1]
+    k1 = t_far / tr[far_inner, 2]
+    m1 = 1.0 / (tr[inner_dev, 0] - t_far * k1)
+    k2 = t_own * m1
+    m2 = 1.0 / (ts[2] - t_own * k2)
+    for cond, cp in pv_in:
+        pl.when(cond)(cp.wait_recv)
+    b1 = pvr[far_inner, 2] + k1 * pvr[far_outer, 2] - pvr[inner_dev, 0]
+    b2 = pvr[inner_dev, 1] - pvr[outer_dev, 2]
+    tile_k1 = jnp.where(left_rows, k1[0:8], k1[CX - 8:CX])
+    for o in others:
+        remote(es, er.at[o], e_ss.at[0], e_rs.at[o], (o, l)).wait_recv()
+
+    def widen(tile):
         full = jnp.concatenate([tile, jnp.zeros((CX - 16, NY), F32), tile], axis=0)
-        jump[k] = jump[k] + jnp.where((row < 2) | (row >= CX - 2), full, 0.0)
-    b0 = jump[0]
-    b1 = jump[1] + k1 * b0
-    b2 = jump[2] + k2 * b1
-    q2 = b2 * m2
-    q1 = b1 * m1 + k2 * q2
-    q0 = b0 * m0 + k1 * q1
-    below = jnp.where(g == 1, q0, jnp.where(g == 2, q1, jnp.where(g == 3, q2, 0.0)))
-    above = jnp.where(g == 0, q0, jnp.where(g == 1, q1, jnp.where(g == 2, q2, 0.0)))
+        return jnp.where((row < 2) | (row >= CX - 2), full, 0.0)
+
+    b1 = b1 + widen(er[far_inner, 2] + tile_k1 * er[far_outer, 2] - er[inner_dev, 0])
+    b2 = b2 + widen(er[inner_dev, 1] - er[outer_dev, 2])
+    r2 = (b2 + k2 * b1) * m2
+    r1 = (b1 + t_own * r2) * m1
+    below = jnp.where(g == 3, r2, jnp.where(g == 2, r1, jnp.where(g == 1, -r2, 0.0)))
+    above = jnp.where(g == 0, -r2, jnp.where(g == 1, -r1, jnp.where(g == 2, r2, 0.0)))
 
     def close(k, _):
         for r in range(BZ):
@@ -436,9 +489,9 @@
 
     lax.fori_loop(0, CZ // BZ, close, 0)
 
-    for cond, cp in x_out + z_out + c_out:
+    for cond, cp in x_out + z_out + c_out + w_out + t_out + pv_out:
         pl.when(cond)(cp.wait_send)
-    for cp in g_out + pv_out + e_out:
+    for _, cp in e_out:
         cp.wait_send()
 
 
@@ -459,20 +512,21 @@
             buf(2, 56), buf(2, 56), buf(2, 56), buf(2, 56),
             buf(2, 40), buf(2, 40), buf(2, 40), buf(2, 40), buf(2, 4, CZ),
             buf(2, 4, CZ), buf(2, 4, CZ),
-            buf(2, 3, CX), buf(2, 3, CX),
+            buf(2, 4, CX), buf(2, 4, CX),
             buf(4, 8), buf(4, 8),
-            buf(5, CX), buf(NG, 5, CX),
-            buf(2, CX), buf(NG, 2, CX),
-            buf(2, 8), buf(NG, 2, 8),
+            buf(3, CX), buf(NG, 3, CX),
+            buf(3, CX), buf(NG, 3, CX),
+            buf(3, 8), buf(NG, 3, 8),
             pltpu.SMEM((1, 1, 6), jnp.int32),
             pltpu.SMEM((1, 1), jnp.int32),
             dma((5,)),
             dma((2,)), dma((2,)),
-            dma((2,)), dma((2,)),
+            dma((4,)), dma((4,)),
             dma((4,)), dma((4,)),
             dma((3,)), dma((NG,)),
             dma((3,)), dma((NG,)),
             dma((3,)), dma((NG,)),
+            pltpu.SemaphoreType.REGULAR,
         ],
         compiler_params=pltpu.CompilerParams(
             collective_id=0, has_side_effects=True, vmem_limit_bytes=66000000

time: 15.8 us -> 14.5 us (0.918)
  Pallas kernels: 14.1 us -> 12.9 us
    pallas_call x1, Pallas kernels: 14.1 us -> 12.9 us  [step(): pl.pallas_call(kernel, out_shape=pltpu.VMEM((CZ, CX, NY), F32), in_specs=...]
where the time goes in v3:
time: 14.5 us; the launch traced here: 14.4 us
  Pallas kernels  12.9 us (89%)
  local copies, waits for them, and re-layouts  0.8 us (6%)
  between operations  0.66 us (5%)
    pallas_call x1, Pallas kernels, step(): pl.pallas_call(kernel, out_shape=pltpu.VMEM((CZ, CX, NY), F32), in_specs=...  12.9 us
    unnamed x1, local copies, waits for them, and re-layouts  0.8 us

profile of v3, /device:TPU:96, one launch (start us, length us, event | category | flops | bytes accessed | tf_op | source)
XLA Modules:
  0.0 14.4 jit_solution(1030065040879926749)
XLA Ops:
  0.7 12.9 %shard_map.55 = f32[32,32,128]{2,1,0:T(8,128)S(1)} custom-call(f32[32,32,128]{2,1,0:T(8,128)} %phase.1, f32[32,32,128]{2,1,0:T(8,128)} %old.1, f32[32,32,128]{2,1,0:T(8,128)} %solute.1, s32[1,1,6]{2,1,0:T(1,128)} %blocks.1, s32[1,1]{1,0:T(1,128)S(6)} %copy.8.count), custom_call_target="tpu_custom_call" | custom-call | tf_op jit(solution)/shard_map/pallas_call | solution.py:504
  13.6 0.8 %copy.7 = f32[32,32,128]{2,1,0:T(8,128)} copy(f32[32,32,128]{2,1,0:T(8,128)S(1)} %shard_map.55) | data formatting | bytes 1048576

commit v4 on v3

--- a/solution.py
+++ b/solution.py
@@ -38,9 +38,9 @@
 def kernel(
     phase, old, solute, blocks, count, out,
     ph, so, po, s0, fx, fz, rh, ee, bb, wf, pf, vb, qf, dd, pp, qq, ea, eb,
-    cin, cnx, cout, cs0, cgy, cgz, cfa, cfz, cpq,
-    xs, xr, zs, zr, cs, cr, ts, tr, pvs, pvr, es, er, blk, cnt,
-    in_sem, x_ss, x_rs, z_ss, z_rs, c_ss, c_rs, t_ss, t_rs, pv_ss, pv_rs, e_ss, e_rs, met,
+    cin, cnx, cout, cs0, cgy, cgz, cfa, cfz, cpq, cgo, w8,
+    xs, xr, zs, zr, cs, cr, ts, tr, ss, sr, pvs, pvr, es, er, blk, cnt,
+    in_sem, x_ss, x_rs, z_ss, z_rs, c_ss, c_rs, t_ss, t_rs, s_ss, s_rs, pv_ss, pv_rs, e_ss, e_rs, met,
 ):
     g = lax.axis_index("growth")
     l = lax.axis_index("lateral")
@@ -117,6 +117,7 @@
         return jnp.where(hit, 0.25, 0.0)
 
     column_mask = masked(row // BZ)
+    sub = lax.broadcasted_iota(jnp.int32, (8, NY), 0)
     for side, x in ((0, 0), (1, CX - 1)):
         near = 1 if x == 0 else CX - 2
         here, s = ph[1:CZ + 1, PAD + x, :], so[:, PAD + x, :]
@@ -128,8 +129,11 @@
         zs[side, 0] = phz(z)
         zs[side, 1] = phz(1 if z == 0 else CZ - 2)
         zs[side, 2] = (1.0 + 0.7 * soz(z)) * (phz(z) - po[z]) * masked(jnp.int32(z // BZ))
-        cs[2 * side] = phz(z)[0:8]
-        cs[2 * side + 1] = phz(z)[CX - 8:CX]
+        for right, x in ((0, 0), (1, CX - 1)):
+            slot = 3 - (2 * side + right)
+            want = (sub // 4 == slot % 2) & (sub % 2 == slot // 2)
+            corner = jnp.broadcast_to(phz(z)[x:x + 1], (8, NY))
+            cs[2 * side + right] = jnp.where(want, corner, 0.0)
 
     def many(*conds):
         return sum(c.astype(jnp.int32) for c in conds)
@@ -161,12 +165,12 @@
         (cond, remote(cs.at[i], cr.at[3 - i], c_ss.at[i], c_rs.at[3 - i], dev))
         for i, (cond, dev) in enumerate(diag)
     ]
-    for cond, cp in z_out + x_out:
-        pl.when(cond)(cp.start)
     for i, (cond, o) in enumerate(((has_lo, g_lo), (has_hi, g_hi))):
         @pl.when(cond)
         def _():
             pl.semaphore_signal(met, inc=1, device_id=(o, l), device_id_type=MESH)
+    for cond, cp in z_out + x_out:
+        pl.when(cond)(cp.start)
     x_in = [
         (has_xl, remote(xs.at[1], xr.at[0], x_ss.at[1], x_rs.at[0], (g, l_lo))),
         (has_xr, remote(xs.at[0], xr.at[1], x_ss.at[0], x_rs.at[1], (g, l_hi))),
@@ -185,27 +189,38 @@
     half = up.astype(jnp.int32)
     inner_dev, outer_dev = 1 + half, 3 * half
     far_inner, far_outer = 2 - half, 3 - 3 * half
-    t_out, pv_out = [], []
+    beside = [(has_lo, g_lo), (has_hi, g_hi)]
+    t_out = [
+        (middle & cond, remote(ts, tr.at[g], t_ss.at[i], t_rs.at[g], (o, l)))
+        for i, (cond, o) in enumerate(beside)
+    ]
+    t_far_out = [(middle, remote(ts, tr.at[g], t_ss.at[2], t_rs.at[g], (far_outer, l)))]
+    t_in = [
+        (cond & (o > 0) & (o < NG - 1), remote(ts, tr.at[o], t_ss.at[0], t_rs.at[o], (o, l)))
+        for cond, o in beside
+    ]
+    t_in.append(
+        (ends, remote(ts, tr.at[far_inner], t_ss.at[0], t_rs.at[far_inner], (far_inner, l)))
+    )
+    s_out, pv_out, e_out = [], [], []
     for d, o in enumerate(others):
         to_end = middle & (o == outer_dev)
         to_far = middle & (o != outer_dev)
-        for cond, at in ((to_end, pl.ds(0, 2)), (to_far, pl.ds(1, 2))):
-            t_out.append((cond, remote(ts.at[at], tr.at[g, at], t_ss.at[d], t_rs.at[g], (o, l))))
+        for cond, at in ((to_end, pl.ds(0, 1)), (to_far, pl.ds(1, 1))):
+            s_out.append((cond, remote(ss.at[at], sr.at[g, at], s_ss.at[d], s_rs.at[g], (o, l))))
         for cond, at in ((to_end, pl.ds(0, 2)), (jnp.logical_not(to_end), pl.ds(2, 1))):
             pv_out.append((cond, remote(pvs.at[at], pvr.at[g, at], pv_ss.at[d], pv_rs.at[g], (o, l))))
-    t_in, pv_in = [], []
+            e_out.append((cond, remote(es.at[at], er.at[g, at], e_ss.at[d], e_rs.at[g], (o, l))))
+    s_in, pv_in, e_in = [], [], []
     for k in range(NG):
-        from_inner = jnp.logical_not(middle) & (inner_dev == k)
+        from_inner = ends & (inner_dev == k)
+        from_other = (g != k) & jnp.logical_not(from_inner)
         if k in (1, 2):
-            from_far = far_inner == k
-            for cond, at in ((from_inner, pl.ds(0, 2)), (from_far, pl.ds(1, 2))):
-                t_in.append((cond, remote(ts.at[at], tr.at[k, at], t_ss.at[0], t_rs.at[k], (k, l))))
-        from_other = (g != k) & jnp.logical_not(from_inner)
+            for cond, at in ((from_inner, pl.ds(0, 1)), (from_other, pl.ds(1, 1))):
+                s_in.append((cond, remote(ss.at[at], sr.at[k, at], s_ss.at[0], s_rs.at[k], (k, l))))
         for cond, at in ((from_inner, pl.ds(0, 2)), (from_other, pl.ds(2, 1))):
             pv_in.append((cond, remote(pvs.at[at], pvr.at[k, at], pv_ss.at[0], pv_rs.at[k], (k, l))))
-    e_out = [
-        (None, remote(es, er.at[g], e_ss.at[d], e_rs.at[g], (o, l))) for d, o in enumerate(others)
-    ]
+            e_in.append((cond, remote(es.at[at], er.at[k, at], e_ss.at[0], e_rs.at[k], (k, l))))
 
     bottom = jnp.where(g == 0, face(phz(0), 0.0), zero) + 1.0
     top = jnp.where(g == NG - 1, face(phz(CZ - 1), 0.0), zero) + 1.0
@@ -252,9 +267,12 @@
     lax.fori_loop(0, CZ // BZ, finish, 0)
     zs[0, 3] = pp[0]
     zs[1, 3] = qq[CZ - 1]
-    ts[1] = pp[CZ - 1]
+    ts[...] = pp[CZ - 1]
+    tr[g] = ts[...]
+    for cond, cp in w_out + t_out:
+        pl.when(cond)(cp.start)
     pl.semaphore_wait(met, many(has_lo, has_hi))
-    for cond, cp in c_out + w_out:
+    for cond, cp in c_out + t_far_out:
         pl.when(cond)(cp.start)
 
 
@@ -336,20 +354,18 @@
         cpq[side, 2] = pp[:, near, :]
         cpq[side, 3] = qq[:, near, :]
 
-    for cond, cp in z_in:
-        pl.when(cond)(cp.wait_recv)
-    for cond, cp in w_in:
+    for cond, cp in z_in + w_in:
         pl.when(cond)(cp.wait_recv)
     self_hi = 1.0 / face(phz(CZ - 1), zr[1, 0]) + qq[CZ - 1] + zr[1, 3]
     self_lo = 1.0 / face(phz(0), zr[0, 0]) + pp[0] + zr[0, 3]
     even = lax.rem(g, 2) == 0
     self_out = jnp.where(even, self_hi, self_lo)
-    ts[0] = jnp.where(even, self_lo, self_hi)
-    ts[2] = self_out
-    tr[g] = ts[...]
-    for cond, cp in t_out:
+    ss[0] = jnp.where(even, self_lo, self_hi)
+    ss[1] = self_out
+    sr[g] = ss[...]
+    for cond, cp in s_out:
         pl.when(cond)(cp.start)
-    own_k = ts[1] / self_out
+    own_k = ts[...] / self_out
     ph[0, pl.ds(PAD, CX), :] = zr[0, 0]
     ph[CZ + 1, pl.ds(PAD, CX), :] = zr[1, 0]
     for side, z in ((0, -1), (1, CZ)):
@@ -371,7 +387,7 @@
 
     for side, x in ((0, 0), (1, CX - 1)):
         near = 1 if x == 0 else CX - 2
-        for buf, which, xx in ((cin, 0, x), (cnx, 0, near), (cs0, 2, x)):
+        for buf, which, xx in ((cin, 0, x), (cnx, 0, near)):
             buf[side, 7:8] = zr[0, which, xx:xx + 1, :]
             buf[side, 40:41] = zr[1, which, xx:xx + 1, :]
         cin[side, 6:7] = zr[0, 1, x:x + 1, :]
@@ -380,26 +396,23 @@
         cgy[side] = next_y(a, last_e) - prev_y(a, first_e)
         cgz[side] = cin[side, 8:48] - cin[side, 6:46]
 
-    for cond, cp in x_in + c_in:
+    for cond, cp in x_in:
         pl.when(cond)(cp.wait_recv)
-    sub = lax.broadcasted_iota(jnp.int32, (8, NY), 0)
     tile_p = jnp.zeros((8, NY), F32)
     tile_q = jnp.zeros((8, NY), F32)
     for side, x in ((0, 0), (1, CX - 1)):
         near = 1 if x == 0 else CX - 2
-        pick = slice(7, 8) if side == 0 else slice(0, 1)
         outer = xr[side, 0]
-        cout[side, 7:8] = cr[side, pick]
         cout[side, 8:40] = outer
-        cout[side, 40:41] = cr[2 + side, pick]
         gin = cnx[side, 7:47] - cout[side, 7:47]
         factor = flux_factor(gin, cgy[side], cgz[side], cs0[side, 7:47])
         cfa[side] = factor
         cfz[side] = factor * cgz[side]
         g_out2 = xs[side, 0] - xr[side, 1]
+        gy_out = ydiff(outer)
         f_out = flux_factor(
-            g_out2, ydiff(outer), cout[side, 9:41] - cout[side, 7:39], xr[side, 3]
-        ) * g_out2
+            g_out2, gy_out, cout[side, 9:41] - cout[side, 7:39], xr[side, 3]
+        ) * jnp.where(inner, g_out2, 0.0)
         own = cfa[side, 1:33]
         d_near = -own * (xs[side, 1] - outer)
         d_edge = (
@@ -414,6 +427,44 @@
             tile_q = jnp.where(sub == where, jnp.sum(cpq[side, k + 1] * d, axis=0, keepdims=True), tile_q)
         cfa[side, 0:32] = d_edge
         cfz[side, 0:32] = d_near
+        cgo[side, 0] = g_out2
+        cgo[side, 1] = gy_out
+        for end, z in ((0, 0), (1, CZ - 1)):
+            at_a, at_b = 4 * side + end, 4 * side + 2 + end
+            zb = 7 if end == 0 else 40
+            inz = 1 if end == 0 else CZ - 2
+            w8[0, at_a:at_a + 1] = xr[side, 0, inz:inz + 1, :]
+            w8[1, at_a:at_a + 1] = cgo[side, 0, z:z + 1]
+            w8[2, at_a:at_a + 1] = cgo[side, 1, z:z + 1]
+            w8[3, at_a:at_a + 1] = -xr[side, 3, z:z + 1, :]
+            w8[0, at_b:at_b + 1] = cnx[side, zb:zb + 1]
+            w8[1, at_b:at_b + 1] = cgz[side, zb - 7:zb - 6]
+            w8[2, at_b:at_b + 1] = cgy[side, zb - 7:zb - 6]
+            w8[3, at_b:at_b + 1] = zr[end, 2, x:x + 1, :] * (-1.0 if end == 0 else 1.0)
+            for at in (at_a, at_b):
+                w8[4, at:at + 1] = cpq[side, 0, z:z + 1]
+                w8[5, at:at + 1] = cpq[side, 1, z:z + 1]
+    carry2 = w8[1] * w8[1]
+    side2 = w8[2] * w8[2]
+    known2 = carry2 + side2 + 1.0
+    known4 = carry2 * carry2 + side2 * side2
+    scale = w8[3] * w8[1]
+    base8, weight_p, weight_q = w8[0], w8[4], w8[5]
+    for cond, cp in c_in:
+        pl.when(cond)(cp.wait_recv)
+    v = base8 - ((cr[0] + cr[1]) + (cr[2] + cr[3]))
+    v2 = v * v
+    inv = lax.rsqrt(known2 + v2)
+    inv2 = inv * inv
+    d8 = scale * inv * (0.1 + 1.2 * (known4 + v2 * v2) * (inv2 * inv2))
+
+    def corner_rows(y):
+        y = y + pltpu.roll(y, 7, 0)
+        y = y + pltpu.roll(y, 6, 0)
+        return jnp.where(sub == 0, y, jnp.where(sub == 7, pltpu.roll(y, 3, 0), 0.0))
+
+    tile_p = tile_p + corner_rows(weight_p * d8)
+    tile_q = tile_q + corner_rows(weight_q * d8)
     left_rows = sub < 4
     tile_facing, tile_away = jnp.where(up, tile_p, tile_q), jnp.where(up, tile_q, tile_p)
     tile_k = jnp.where(left_rows, own_k[0:8], own_k[CX - 8:CX])
@@ -421,8 +472,13 @@
     es[1] = tile_away
     es[2] = jnp.where(middle, tile_facing - tile_k * tile_away, tile_facing)
     er[g] = es[...]
-    for _, cp in e_out:
-        cp.start()
+    for cond, cp in e_out:
+        pl.when(cond)(cp.start)
+    w8[0] = d8
+    for side in (0, 1):
+        for end, z in ((0, 0), (1, CZ - 1)):
+            at_a, at_b = 4 * side + end, 4 * side + 2 + end
+            cfa[side, z:z + 1] = cfa[side, z:z + 1] + w8[0, at_a:at_a + 1] + w8[0, at_b:at_b + 1]
     for side, x in ((0, 0), (1, CX - 1)):
         near = 1 if x == 0 else CX - 2
         rh[:, x, :] = rh[:, x, :] + cfa[side, 0:32]
@@ -455,20 +511,19 @@
 
     lax.fori_loop(0, CZ // BZ, local, 0)
 
-    for cond, cp in t_in:
+    for cond, cp in t_in + s_in + pv_in:
         pl.when(cond)(cp.wait_recv)
-    t_far, t_own = tr[far_inner, 1], tr[inner_dev, 1]
-    k1 = t_far / tr[far_inner, 2]
-    m1 = 1.0 / (tr[inner_dev, 0] - t_far * k1)
+    t_far = tr[far_inner]
+    t_own = tr[inner_dev]
+    k1 = t_far / sr[far_inner, 1]
+    m1 = 1.0 / (sr[inner_dev, 0] - t_far * k1)
     k2 = t_own * m1
-    m2 = 1.0 / (ts[2] - t_own * k2)
-    for cond, cp in pv_in:
-        pl.when(cond)(cp.wait_recv)
+    m2 = 1.0 / (ss[1] - t_own * k2)
     b1 = pvr[far_inner, 2] + k1 * pvr[far_outer, 2] - pvr[inner_dev, 0]
     b2 = pvr[inner_dev, 1] - pvr[outer_dev, 2]
     tile_k1 = jnp.where(left_rows, k1[0:8], k1[CX - 8:CX])
-    for o in others:
-        remote(es, er.at[o], e_ss.at[0], e_rs.at[o], (o, l)).wait_recv()
+    for cond, cp in e_in:
+        pl.when(cond)(cp.wait_recv)
 
     def widen(tile):
         full = jnp.concatenate([tile, jnp.zeros((CX - 16, NY), F32), tile], axis=0)
@@ -489,10 +544,8 @@
 
     lax.fori_loop(0, CZ // BZ, close, 0)
 
-    for cond, cp in x_out + z_out + c_out + w_out + t_out + pv_out:
+    for cond, cp in x_out + z_out + c_out + w_out + t_out + t_far_out + s_out + pv_out + e_out:
         pl.when(cond)(cp.wait_send)
-    for _, cp in e_out:
-        cp.wait_send()
 
 
 def step(phase, old, solute, blocks, count):
@@ -511,10 +564,12 @@
             slab, slab, slab, slab, slab, slab, slab, slab, slab, slab, slab, slab,
             buf(2, 56), buf(2, 56), buf(2, 56), buf(2, 56),
             buf(2, 40), buf(2, 40), buf(2, 40), buf(2, 40), buf(2, 4, CZ),
+            buf(2, 2, CZ), buf(6, 8),
             buf(2, 4, CZ), buf(2, 4, CZ),
             buf(2, 4, CX), buf(2, 4, CX),
             buf(4, 8), buf(4, 8),
-            buf(3, CX), buf(NG, 3, CX),
+            buf(CX), buf(NG, CX),
+            buf(2, CX), buf(NG, 2, CX),
             buf(3, CX), buf(NG, 3, CX),
             buf(3, 8), buf(NG, 3, 8),
             pltpu.SMEM((1, 1, 6), jnp.int32),
@@ -526,6 +581,7 @@
             dma((3,)), dma((NG,)),
             dma((3,)), dma((NG,)),
             dma((3,)), dma((NG,)),
+            dma((3,)), dma((NG,)),
             pltpu.SemaphoreType.REGULAR,
         ],
         compiler_params=pltpu.CompilerParams(

time: 14.5 us -> 13.9 us (0.959)
  Pallas kernels: 12.9 us -> 12.3 us
    pallas_call x1, Pallas kernels: 12.9 us -> 12.3 us  [step(): pl.pallas_call(kernel, out_shape=pltpu.VMEM((CZ, CX, NY), F32), in_specs=...]
where the time goes in v4:
time: 13.9 us; the launch traced here: 13.7 us
  Pallas kernels  12.3 us (88%)
  local copies, waits for them, and re-layouts  0.8 us (6%)
  between operations  0.66 us (5%)
    pallas_call x1, Pallas kernels, step(): pl.pallas_call(kernel, out_shape=pltpu.VMEM((CZ, CX, NY), F32), in_specs=...  12.3 us
    unnamed x1, local copies, waits for them, and re-layouts  0.8 us

profile of v4, /device:TPU:96, one launch (start us, length us, event | category | flops | bytes accessed | tf_op | source)
XLA Modules:
  0.0 13.7 jit_solution(13491354061190258682)
XLA Ops:
  0.7 12.3 %shard_map.55 = f32[32,32,128]{2,1,0:T(8,128)S(1)} custom-call(f32[32,32,128]{2,1,0:T(8,128)} %phase.1, f32[32,32,128]{2,1,0:T(8,128)} %old.1, f32[32,32,128]{2,1,0:T(8,128)} %solute.1, s32[1,1,6]{2,1,0:T(1,128)} %blocks.1, s32[1,1]{1,0:T(1,128)S(6)} %copy.8.count), custom_call_target="tpu_custom_call" | custom-call | tf_op jit(solution)/shard_map/pallas_call | solution.py:557
  12.9 0.8 %copy.7 = f32[32,32,128]{2,1,0:T(8,128)} copy(f32[32,32,128]{2,1,0:T(8,128)S(1)} %shard_map.55) | data formatting | bytes 1048576

commit v5 on v4

--- a/solution.py
+++ b/solution.py
@@ -36,8 +36,8 @@
 
 
 def kernel(
-    phase, old, solute, blocks, count, out,
-    ph, so, po, s0, fx, fz, rh, ee, bb, wf, pf, vb, qf, dd, pp, qq, ea, eb,
+    phase, old, solute, blocks, count, ee, pp, qq, below_out, above_out,
+    ph, so, po, s0, fx, fz, rh, bb, wf, pf, vb, qf, dd, ea, eb,
     cin, cnx, cout, cs0, cgy, cgz, cfa, cfz, cpq, cgo, w8,
     xs, xr, zs, zr, cs, cr, ts, tr, ss, sr, pvs, pvr, es, er, blk, cnt,
     in_sem, x_ss, x_rs, z_ss, z_rs, c_ss, c_rs, t_ss, t_rs, s_ss, s_rs, pv_ss, pv_rs, e_ss, e_rs, met,
@@ -395,6 +395,18 @@
         a = cin[side, 7:47]
         cgy[side] = next_y(a, last_e) - prev_y(a, first_e)
         cgz[side] = cin[side, 8:48] - cin[side, 6:46]
+
+    for side, x in ((0, 0), (1, CX - 1)):
+        for end, z in ((0, 0), (1, CZ - 1)):
+            at_a, at_b = 4 * side + end, 4 * side + 2 + end
+            zb = 7 if end == 0 else 40
+            w8[0, at_b:at_b + 1] = cnx[side, zb:zb + 1]
+            w8[1, at_b:at_b + 1] = cgz[side, zb - 7:zb - 6]
+            w8[2, at_b:at_b + 1] = cgy[side, zb - 7:zb - 6]
+            w8[3, at_b:at_b + 1] = zr[end, 2, x:x + 1, :] * (-1.0 if end == 0 else 1.0)
+            for at in (at_a, at_b):
+                w8[4, at:at + 1] = cpq[side, 0, z:z + 1]
+                w8[5, at:at + 1] = cpq[side, 1, z:z + 1]
 
     for cond, cp in x_in:
         pl.when(cond)(cp.wait_recv)
@@ -431,19 +443,11 @@
         cgo[side, 1] = gy_out
         for end, z in ((0, 0), (1, CZ - 1)):
             at_a, at_b = 4 * side + end, 4 * side + 2 + end
-            zb = 7 if end == 0 else 40
             inz = 1 if end == 0 else CZ - 2
             w8[0, at_a:at_a + 1] = xr[side, 0, inz:inz + 1, :]
             w8[1, at_a:at_a + 1] = cgo[side, 0, z:z + 1]
             w8[2, at_a:at_a + 1] = cgo[side, 1, z:z + 1]
             w8[3, at_a:at_a + 1] = -xr[side, 3, z:z + 1, :]
-            w8[0, at_b:at_b + 1] = cnx[side, zb:zb + 1]
-            w8[1, at_b:at_b + 1] = cgz[side, zb - 7:zb - 6]
-            w8[2, at_b:at_b + 1] = cgy[side, zb - 7:zb - 6]
-            w8[3, at_b:at_b + 1] = zr[end, 2, x:x + 1, :] * (-1.0 if end == 0 else 1.0)
-            for at in (at_a, at_b):
-                w8[4, at:at + 1] = cpq[side, 0, z:z + 1]
-                w8[5, at:at + 1] = cpq[side, 1, z:z + 1]
     carry2 = w8[1] * w8[1]
     side2 = w8[2] * w8[2]
     known2 = carry2 + side2 + 1.0
@@ -536,13 +540,8 @@
     below = jnp.where(g == 3, r2, jnp.where(g == 2, r1, jnp.where(g == 1, -r2, 0.0)))
     above = jnp.where(g == 0, -r2, jnp.where(g == 1, -r1, jnp.where(g == 2, r2, 0.0)))
 
-    def close(k, _):
-        for r in range(BZ):
-            z = k * BZ + r
-            out[z] = ee[z] + pp[z] * below - qq[z] * above
-        return 0
-
-    lax.fori_loop(0, CZ // BZ, close, 0)
+    below_out[...] = below
+    above_out[...] = above
 
     for cond, cp in x_out + z_out + c_out + w_out + t_out + t_far_out + s_out + pv_out + e_out:
         pl.when(cond)(cp.wait_send)
@@ -554,14 +553,14 @@
 
     slab = buf(CZ, CX)
     dma = pltpu.SemaphoreType.DMA
-    return pl.pallas_call(
+    parts = pl.pallas_call(
         kernel,
-        out_shape=pltpu.VMEM((CZ, CX, NY), F32),
+        out_shape=[pltpu.VMEM((CZ, CX, NY), F32)] * 3 + [pltpu.VMEM((CX, NY), F32)] * 2,
         in_specs=[pl.BlockSpec(memory_space=pl.ANY)] * 5,
-        out_specs=pl.BlockSpec(memory_space=pltpu.VMEM),
+        out_specs=[pl.BlockSpec(memory_space=pltpu.VMEM)] * 5,
         scratch_shapes=[
             buf(CZ + 2, ROW), buf(CZ, ROW), slab, slab, buf(CZ, ROW), buf(CZ + 2, CX),
-            slab, slab, slab, slab, slab, slab, slab, slab, slab, slab, slab, slab,
+            slab, slab, slab, slab, slab, slab, slab, slab, slab,
             buf(2, 56), buf(2, 56), buf(2, 56), buf(2, 56),
             buf(2, 40), buf(2, 40), buf(2, 40), buf(2, 40), buf(2, 4, CZ),
             buf(2, 2, CZ), buf(6, 8),
@@ -585,9 +584,32 @@
             pltpu.SemaphoreType.REGULAR,
         ],
         compiler_params=pltpu.CompilerParams(
-            collective_id=0, has_side_effects=True, vmem_limit_bytes=66000000
+            collective_id=0, has_side_effects=True, vmem_limit_bytes=65400000
         ),
     )(phase, old, solute, blocks, count)
+    chunks = 4
+    deep = CZ // chunks
+
+    def close(ee, pp, qq, below, above, dst, stage, sems):
+        lo, hi = below[...], above[...]
+        cps = []
+        for c in range(chunks):
+            for z in range(c * deep, (c + 1) * deep):
+                stage[z] = ee[z] + pp[z] * lo - qq[z] * hi
+            at = pl.ds(c * deep, deep)
+            cps.append(pltpu.make_async_copy(stage.at[at], dst.at[at], sems.at[c]))
+            cps[-1].start()
+        for cp in cps:
+            cp.wait()
+
+    return pl.pallas_call(
+        close,
+        out_shape=jax.ShapeDtypeStruct((CZ, CX, NY), F32),
+        in_specs=[pl.BlockSpec(memory_space=pltpu.VMEM)] * 5,
+        out_specs=pl.BlockSpec(memory_space=pl.ANY),
+        scratch_shapes=[slab, dma((chunks,))],
+        compiler_params=pltpu.CompilerParams(vmem_limit_bytes=4194304),
+    )(*[pltpu.with_memory_space_constraint(a, pltpu.VMEM) for a in parts])
 
 
 def solution(mesh):

time: 13.9 us -> 13.9 us (level)
  local copies, waits for them, and re-layouts: 0.8 us -> 0 us
  Pallas kernels: 12.3 us -> 13 us
    unnamed x1 -> x0, local copies, waits for them, and re-layouts: 0.8 us -> none
    pallas_call x1 -> x2, Pallas kernels: 12.3 us -> 13 us  [the longest x1 12.2 us: step(): pl.pallas_call(kernel, out_shape=[pltpu.VMEM((CZ, CX, NY), F32)] * 3 + [p...]
where the time goes in v5:
time: 13.9 us; the launch traced here: 13.7 us
  Pallas kernels  13 us (94%)
  between operations  0.66 us (5%)
    pallas_call x1, Pallas kernels, step(): pl.pallas_call(kernel, out_shape=[pltpu.VMEM((CZ, CX, NY), F32)] * 3 + [p...  12.2 us
    pallas_call x1, Pallas kernels, step(): pl.pallas_call(close, out_shape=jax.ShapeDtypeStruct((CZ, CX, NY), F32),...  0.84 us

profile of v5, /device:TPU:96, one launch (start us, length us, event | category | flops | bytes accessed | tf_op | source)
XLA Modules:
  0.0 13.7 jit_solution(12603367508847356068)
XLA Ops:
  0.7 12.2 %shard_map.55 = (f32[32,32,128]{2,1,0:T(8,128)S(1)}, f32[32,32,128]{2,1,0:T(8,128)S(1)}, f32[32,32,128]{2,1,0:T(8,128)S(1)}, f32[32,128]{1,0:T(8,128)S(1)}, f32[32,128]{1,0:T(8,128)S(1)}) custom-call(f32[32,32,128]{2,1,0:T(8,128)} %phase.1, f32[32,32,128]{2,1,0:T(8,128)} %old.1, f32[32,32,128]{2,1,0:T(8,128)} %solute.1, s32[1,1,6]{2,1,0:T(1,128)} %blocks.1, ...), custom_call_target="tpu_custom_call" | custom-call | tf_op jit(solution)/shard_map/pallas_call | solution.py:556
  12.8 0.8 %shard_map.56 = f32[32,32,128]{2,1,0:T(8,128)} custom-call(f32[32,32,128]{2,1,0:T(8,128)S(1)} %get-tuple-element.10.ee, f32[32,32,128]{2,1,0:T(8,128)S(1)} %get-tuple-element.11.pp, f32[32,32,128]{2,1,0:T(8,128)S(1)} %get-tuple-element.12.qq, f32[32,128]{1,0:T(8,128)S(1)} %get-tuple-element.13.below, f32[32,128]{1,0:T(8,128)S(1)} %get-tuple-element.14.above), custom_call_target="tpu_custom_call" | custom-call | tf_op jit(solution)/shard_map/pallas_call | solution.py:605

commit v6 on v5

--- a/solution.py
+++ b/solution.py
@@ -526,6 +526,8 @@
     b1 = pvr[far_inner, 2] + k1 * pvr[far_outer, 2] - pvr[inner_dev, 0]
     b2 = pvr[inner_dev, 1] - pvr[outer_dev, 2]
     tile_k1 = jnp.where(left_rows, k1[0:8], k1[CX - 8:CX])
+    for cond, cp in x_out + z_out + c_out + w_out + t_out + t_far_out + s_out + pv_out + e_out:
+        pl.when(cond)(cp.wait_send)
     for cond, cp in e_in:
         pl.when(cond)(cp.wait_recv)
 
@@ -542,9 +544,6 @@
 
     below_out[...] = below
     above_out[...] = above
-
-    for cond, cp in x_out + z_out + c_out + w_out + t_out + t_far_out + s_out + pv_out + e_out:
-        pl.when(cond)(cp.wait_send)
 
 
 def step(phase, old, solute, blocks, count):

time: 13.9 us -> 13.8 us (level)
  no operation moved by 1% of the time
where the time goes in v6:
time: 13.8 us; the launch traced here: 13.6 us
  Pallas kernels  13 us (94%)
  between operations  0.66 us (5%)
    pallas_call x1, Pallas kernels, step(): pl.pallas_call(kernel, out_shape=[pltpu.VMEM((CZ, CX, NY), F32)] * 3 + [p...  12.1 us
    pallas_call x1, Pallas kernels, step(): pl.pallas_call(close, out_shape=jax.ShapeDtypeStruct((CZ, CX, NY), F32),...  0.84 us

profile of v6, /device:TPU:96, one launch (start us, length us, event | category | flops | bytes accessed | tf_op | source)
XLA Modules:
  0.0 13.6 jit_solution(1166992079864234946)
XLA Ops:
  0.7 12.1 %shard_map.55 = (f32[32,32,128]{2,1,0:T(8,128)S(1)}, f32[32,32,128]{2,1,0:T(8,128)S(1)}, f32[32,32,128]{2,1,0:T(8,128)S(1)}, f32[32,128]{1,0:T(8,128)S(1)}, f32[32,128]{1,0:T(8,128)S(1)}) custom-call(f32[32,32,128]{2,1,0:T(8,128)} %phase.1, f32[32,32,128]{2,1,0:T(8,128)} %old.1, f32[32,32,128]{2,1,0:T(8,128)} %solute.1, s32[1,1,6]{2,1,0:T(1,128)} %blocks.1, ...), custom_call_target="tpu_custom_call" | custom-call | tf_op jit(solution)/shard_map/pallas_call | solution.py:555
  12.8 0.8 %shard_map.56 = f32[32,32,128]{2,1,0:T(8,128)} custom-call(f32[32,32,128]{2,1,0:T(8,128)S(1)} %get-tuple-element.10.ee, f32[32,32,128]{2,1,0:T(8,128)S(1)} %get-tuple-element.11.pp, f32[32,32,128]{2,1,0:T(8,128)S(1)} %get-tuple-element.12.qq, f32[32,128]{1,0:T(8,128)S(1)} %get-tuple-element.13.below, f32[32,128]{1,0:T(8,128)S(1)} %get-tuple-element.14.above), custom_call_target="tpu_custom_call" | custom-call | tf_op jit(solution)/shard_map/pallas_call | solution.py:604

commit v7 on v6

--- a/solution.py
+++ b/solution.py
@@ -48,7 +48,7 @@
     has_xl, has_xr = l > 0, l < NL - 1
     g_lo, g_hi = jnp.maximum(g - 1, 0), jnp.minimum(g + 1, NG - 1)
     l_lo, l_hi = jnp.maximum(l - 1, 0), jnp.minimum(l + 1, NL - 1)
-    others = [lax.rem(g + d, NG) for d in (2, 1, 3)]
+    others = [lax.rem(g + d, NG) for d in (2, 3, 1)]
 
     barrier = pltpu.get_barrier_semaphore()
 
@@ -130,10 +130,7 @@
         zs[side, 1] = phz(1 if z == 0 else CZ - 2)
         zs[side, 2] = (1.0 + 0.7 * soz(z)) * (phz(z) - po[z]) * masked(jnp.int32(z // BZ))
         for right, x in ((0, 0), (1, CX - 1)):
-            slot = 3 - (2 * side + right)
-            want = (sub // 4 == slot % 2) & (sub % 2 == slot // 2)
-            corner = jnp.broadcast_to(phz(z)[x:x + 1], (8, NY))
-            cs[2 * side + right] = jnp.where(want, corner, 0.0)
+            cs[2 * side + right] = phz(z)[x:x + 1]
 
     def many(*conds):
         return sum(c.astype(jnp.int32) for c in conds)
@@ -293,7 +290,7 @@
     for i, (cond, _) in enumerate(diag):
         @pl.when(jnp.logical_not(cond))
         def _():
-            cr[i] = jnp.zeros((8, NY), F32)
+            cr[i] = jnp.zeros((1, NY), F32)
 
     def prefactor(k, _):
         mask = masked(k)
@@ -456,7 +453,11 @@
     base8, weight_p, weight_q = w8[0], w8[4], w8[5]
     for cond, cp in c_in:
         pl.when(cond)(cp.wait_recv)
-    v = base8 - ((cr[0] + cr[1]) + (cr[2] + cr[3]))
+    lower, left_half = sub % 2 == 0, sub // 4 == 0
+    corner = [jnp.broadcast_to(cr[i], (8, NY)) for i in range(4)]
+    v = base8 - jnp.where(
+        lower, jnp.where(left_half, corner[0], corner[1]), jnp.where(left_half, corner[2], corner[3])
+    )
     v2 = v * v
     inv = lax.rsqrt(known2 + v2)
     inv2 = inv * inv
@@ -565,7 +566,7 @@
             buf(2, 2, CZ), buf(6, 8),
             buf(2, 4, CZ), buf(2, 4, CZ),
             buf(2, 4, CX), buf(2, 4, CX),
-            buf(4, 8), buf(4, 8),
+            buf(4, 1), buf(4, 1),
             buf(CX), buf(NG, CX),
             buf(2, CX), buf(NG, 2, CX),
             buf(3, CX), buf(NG, 3, CX),

time: 13.8 us -> 13.6 us (0.986)
  Pallas kernels: 13 us -> 12.8 us
where the time goes in v7:
time: 13.6 us; the launch traced here: 13.5 us
  Pallas kernels  12.8 us (94%)
  between operations  0.66 us (5%)
    pallas_call x1, Pallas kernels, step(): pl.pallas_call(kernel, out_shape=[pltpu.VMEM((CZ, CX, NY), F32)] * 3 + [p...  12 us
    pallas_call x1, Pallas kernels, step(): pl.pallas_call(close, out_shape=jax.ShapeDtypeStruct((CZ, CX, NY), F32),...  0.84 us

profile of v7, /device:TPU:96, one launch (start us, length us, event | category | flops | bytes accessed | tf_op | source)
XLA Modules:
  0.0 13.5 jit_solution(15835480098927582086)
XLA Ops:
  0.7 12.0 %shard_map.55 = (f32[32,32,128]{2,1,0:T(8,128)S(1)}, f32[32,32,128]{2,1,0:T(8,128)S(1)}, f32[32,32,128]{2,1,0:T(8,128)S(1)}, f32[32,128]{1,0:T(8,128)S(1)}, f32[32,128]{1,0:T(8,128)S(1)}) custom-call(f32[32,32,128]{2,1,0:T(8,128)} %phase.1, f32[32,32,128]{2,1,0:T(8,128)} %old.1, f32[32,32,128]{2,1,0:T(8,128)} %solute.1, s32[1,1,6]{2,1,0:T(1,128)} %blocks.1, ...), custom_call_target="tpu_custom_call" | custom-call | tf_op jit(solution)/shard_map/pallas_call | solution.py:556
  12.6 0.8 %shard_map.56 = f32[32,32,128]{2,1,0:T(8,128)} custom-call(f32[32,32,128]{2,1,0:T(8,128)S(1)} %get-tuple-element.10.ee, f32[32,32,128]{2,1,0:T(8,128)S(1)} %get-tuple-element.11.pp, f32[32,32,128]{2,1,0:T(8,128)S(1)} %get-tuple-element.12.qq, f32[32,128]{1,0:T(8,128)S(1)} %get-tuple-element.13.below, f32[32,128]{1,0:T(8,128)S(1)} %get-tuple-element.14.above), custom_call_target="tpu_custom_call" | custom-call | tf_op jit(solution)/shard_map/pallas_call | solution.py:605

commit v8 on v7

--- a/solution.py
+++ b/solution.py
@@ -395,7 +395,7 @@
 
     for side, x in ((0, 0), (1, CX - 1)):
         for end, z in ((0, 0), (1, CZ - 1)):
-            at_a, at_b = 4 * side + end, 4 * side + 2 + end
+            at_a, at_b = 2 * end + side, 4 + 2 * end + side
             zb = 7 if end == 0 else 40
             w8[0, at_b:at_b + 1] = cnx[side, zb:zb + 1]
             w8[1, at_b:at_b + 1] = cgz[side, zb - 7:zb - 6]
@@ -439,7 +439,7 @@
         cgo[side, 0] = g_out2
         cgo[side, 1] = gy_out
         for end, z in ((0, 0), (1, CZ - 1)):
-            at_a, at_b = 4 * side + end, 4 * side + 2 + end
+            at_a, at_b = 2 * end + side, 4 + 2 * end + side
             inz = 1 if end == 0 else CZ - 2
             w8[0, at_a:at_a + 1] = xr[side, 0, inz:inz + 1, :]
             w8[1, at_a:at_a + 1] = cgo[side, 0, z:z + 1]
@@ -453,7 +453,7 @@
     base8, weight_p, weight_q = w8[0], w8[4], w8[5]
     for cond, cp in c_in:
         pl.when(cond)(cp.wait_recv)
-    lower, left_half = sub % 2 == 0, sub // 4 == 0
+    lower, left_half = (sub // 2) % 2 == 0, sub % 2 == 0
     corner = [jnp.broadcast_to(cr[i], (8, NY)) for i in range(4)]
     v = base8 - jnp.where(
         lower, jnp.where(left_half, corner[0], corner[1]), jnp.where(left_half, corner[2], corner[3])
@@ -464,9 +464,9 @@
     d8 = scale * inv * (0.1 + 1.2 * (known4 + v2 * v2) * (inv2 * inv2))
 
     def corner_rows(y):
-        y = y + pltpu.roll(y, 7, 0)
-        y = y + pltpu.roll(y, 6, 0)
-        return jnp.where(sub == 0, y, jnp.where(sub == 7, pltpu.roll(y, 3, 0), 0.0))
+        y = y + pltpu.roll(y, 4, 0)
+        y = y + pltpu.roll(y, 2, 0)
+        return jnp.where((sub == 0) | (sub == 7), y, 0.0)
 
     tile_p = tile_p + corner_rows(weight_p * d8)
     tile_q = tile_q + corner_rows(weight_q * d8)
@@ -482,7 +482,7 @@
     w8[0] = d8
     for side in (0, 1):
         for end, z in ((0, 0), (1, CZ - 1)):
-            at_a, at_b = 4 * side + end, 4 * side + 2 + end
+            at_a, at_b = 2 * end + side, 4 + 2 * end + side
             cfa[side, z:z + 1] = cfa[side, z:z + 1] + w8[0, at_a:at_a + 1] + w8[0, at_b:at_b + 1]
     for side, x in ((0, 0), (1, CX - 1)):
         near = 1 if x == 0 else CX - 2

time: 13.6 us -> 13.6 us (level)
  no operation moved by 1% of the time
where the time goes in v8:
time: 13.6 us; the launch traced here: 13.5 us
  Pallas kernels  12.8 us (94%)
  between operations  0.66 us (5%)
    pallas_call x1, Pallas kernels, step(): pl.pallas_call(kernel, out_shape=[pltpu.VMEM((CZ, CX, NY), F32)] * 3 + [p...  12 us
    pallas_call x1, Pallas kernels, step(): pl.pallas_call(close, out_shape=jax.ShapeDtypeStruct((CZ, CX, NY), F32),...  0.84 us

profile of v8, /device:TPU:96, one launch (start us, length us, event | category | flops | bytes accessed | tf_op | source)
XLA Modules:
  0.0 13.5 jit_solution(4668464280415620977)
XLA Ops:
  0.7 12.0 %shard_map.55 = (f32[32,32,128]{2,1,0:T(8,128)S(1)}, f32[32,32,128]{2,1,0:T(8,128)S(1)}, f32[32,32,128]{2,1,0:T(8,128)S(1)}, f32[32,128]{1,0:T(8,128)S(1)}, f32[32,128]{1,0:T(8,128)S(1)}) custom-call(f32[32,32,128]{2,1,0:T(8,128)} %phase.1, f32[32,32,128]{2,1,0:T(8,128)} %old.1, f32[32,32,128]{2,1,0:T(8,128)} %solute.1, s32[1,1,6]{2,1,0:T(1,128)} %blocks.1, ...), custom_call_target="tpu_custom_call" | custom-call | tf_op jit(solution)/shard_map/pallas_call | solution.py:556
  12.6 0.8 %shard_map.56 = f32[32,32,128]{2,1,0:T(8,128)} custom-call(f32[32,32,128]{2,1,0:T(8,128)S(1)} %get-tuple-element.10.ee, f32[32,32,128]{2,1,0:T(8,128)S(1)} %get-tuple-element.11.pp, f32[32,32,128]{2,1,0:T(8,128)S(1)} %get-tuple-element.12.qq, f32[32,128]{1,0:T(8,128)S(1)} %get-tuple-element.13.below, f32[32,128]{1,0:T(8,128)S(1)} %get-tuple-element.14.above), custom_call_target="tpu_custom_call" | custom-call | tf_op jit(solution)/shard_map/pallas_call | solution.py:605

commit v9 on v7

--- a/solution.py
+++ b/solution.py
@@ -266,10 +266,10 @@
     zs[1, 3] = qq[CZ - 1]
     ts[...] = pp[CZ - 1]
     tr[g] = ts[...]
-    for cond, cp in w_out + t_out:
+    for cond, cp in w_out:
         pl.when(cond)(cp.start)
     pl.semaphore_wait(met, many(has_lo, has_hi))
-    for cond, cp in c_out + t_far_out:
+    for cond, cp in c_out:
         pl.when(cond)(cp.start)
 
 
@@ -333,6 +333,8 @@
         return 0
 
     lax.fori_loop(0, 5, planes, 0)
+    for cond, cp in t_out + t_far_out:
+        pl.when(cond)(cp.start)
 
     def rows(k, sums):
         for r in range(BZ):

time: 13.6 us -> 13.6 us (level)
  no operation moved by 1% of the time
where the time goes in v9:
time: 13.6 us; the launch traced here: 13.5 us
  Pallas kernels  12.8 us (94%)
  between operations  0.66 us (5%)
    pallas_call x1, Pallas kernels, step(): pl.pallas_call(kernel, out_shape=[pltpu.VMEM((CZ, CX, NY), F32)] * 3 + [p...  12 us
    pallas_call x1, Pallas kernels, step(): pl.pallas_call(close, out_shape=jax.ShapeDtypeStruct((CZ, CX, NY), F32),...  0.84 us

profile of v9, /device:TPU:96, one launch (start us, length us, event | category | flops | bytes accessed | tf_op | source)
XLA Modules:
  0.0 13.5 jit_solution(9117026380204599172)
XLA Ops:
  0.7 12.0 %shard_map.55 = (f32[32,32,128]{2,1,0:T(8,128)S(1)}, f32[32,32,128]{2,1,0:T(8,128)S(1)}, f32[32,32,128]{2,1,0:T(8,128)S(1)}, f32[32,128]{1,0:T(8,128)S(1)}, f32[32,128]{1,0:T(8,128)S(1)}) custom-call(f32[32,32,128]{2,1,0:T(8,128)} %phase.1, f32[32,32,128]{2,1,0:T(8,128)} %old.1, f32[32,32,128]{2,1,0:T(8,128)} %solute.1, s32[1,1,6]{2,1,0:T(1,128)} %blocks.1, ...), custom_call_target="tpu_custom_call" | custom-call | tf_op jit(solution)/shard_map/pallas_call | solution.py:558
  12.6 0.8 %shard_map.56 = f32[32,32,128]{2,1,0:T(8,128)} custom-call(f32[32,32,128]{2,1,0:T(8,128)S(1)} %get-tuple-element.10.ee, f32[32,32,128]{2,1,0:T(8,128)S(1)} %get-tuple-element.11.pp, f32[32,32,128]{2,1,0:T(8,128)S(1)} %get-tuple-element.12.qq, f32[32,128]{1,0:T(8,128)S(1)} %get-tuple-element.13.below, f32[32,128]{1,0:T(8,128)S(1)} %get-tuple-element.14.above), custom_call_target="tpu_custom_call" | custom-call | tf_op jit(solution)/shard_map/pallas_call | solution.py:607
